TPU v7x, 256 devices: a whole 4x4x8 slice. The times are simulated.
256 devices in a mesh: gx: 16 (over z, y_lo), gy: 16 (over x, y_hi, core).
Axes of the slice: x: 4, y: 4 (y_hi: 2, y_lo: 2; y = y_hi * 2 + y_lo), z: 8, core: 2. Of those that a mesh axis runs over, the one named last changes fastest.
Arguments:
- field_slab: bfloat16 [1536, 256, 64], P('gx', 'gy'), may hold values from -6 to 6
- one_by_second: bfloat16 [256, 400], P('gy'), may hold values from -0.375 to 0.375
- one_by_hours: bfloat16 [64, 400], replicated, may hold values from -0.75 to 0.75
- two_by_first: bfloat16 [1536, 400], P('gx'), may hold values from -0.15625 to 0.15625
- two_by_hours: bfloat16 [64, 400], replicated, may hold values from -0.75 to 0.75
- three_by_first: bfloat16 [1536, 400], P('gx'), may hold values from -0.15625 to 0.15625
- three_by_second: bfloat16 [256, 400], P('gy'), may hold values from -0.375 to 0.375
- core_first: bfloat16 [800, 1536], P(None, 'gx'), may hold values from -0.15625 to 0.15625
- core_second: bfloat16 [800, 256], P(None, 'gy'), may hold values from -0.375 to 0.375
- core_hours: bfloat16 [800, 64], replicated, may hold values from -0.75 to 0.75
Outputs:
- mode_one: float32 [1536, 400], P(('gx', 'gy'))
- mode_two: float32 [256, 400], P('gy')
- mode_three: float32 [64, 400], replicated
- core_sketch: float32 [800, 800, 800], P('gx', 'gy')
All inputs are finite; a program needn't handle non-finite values.
Results may differ from a plain program's by a relative error of at most 0.0041.
Values may be sent and summed in bfloat16 or wider, within the bound.
A program may use at most 64 MiB of HBM per device.

v0:
```python
import jax
import jax.numpy as jnp
from jax import lax
from jax.sharding import PartitionSpec as P


def outer_test(left_factor, right_factor):
    return (
        left_factor.astype(jnp.float32)[:, None, :] * right_factor.astype(jnp.float32)[None, :, :]
    ).astype(jnp.bfloat16)


def on_device(
    field_slab,
    one_by_second,
    one_by_hours,
    two_by_first,
    two_by_hours,
    three_by_first,
    three_by_second,
    core_first,
    core_second,
    core_hours,
):
    rows_here, cols_here, hour_count = field_slab.shape
    sketch_width = one_by_hours.shape[1]
    core_side = core_hours.shape[0]
    flat_field = field_slab.reshape(rows_here, cols_here * hour_count)
    test_one = outer_test(one_by_second, one_by_hours).reshape(cols_here * hour_count, sketch_width)
    first_part = jnp.dot(flat_field, test_one, preferred_element_type=jnp.float32)
    test_two = outer_test(two_by_first, two_by_hours)
    second_part = jnp.einsum(
        "ijt,itk->jk", field_slab, test_two, preferred_element_type=jnp.float32
    )

    def hour_block(block_index, summed):
        offset = block_index * 8
        row_block = lax.dynamic_slice_in_dim(field_slab, offset, 8, 0).reshape(
            8 * cols_here, hour_count
        )
        first_rows = lax.dynamic_slice_in_dim(three_by_first, offset, 8, 0)
        test_three = outer_test(first_rows, three_by_second).reshape(8 * cols_here, sketch_width)
        return summed + lax.dot_general(
            row_block, test_three, (((0,), (0,)), ((), ())), preferred_element_type=jnp.float32
        )

    hour_part = lax.fori_loop(
        0, rows_here // 8, hour_block, jnp.zeros((hour_count, sketch_width), jnp.float32)
    )
    whole_rows = lax.psum(first_part, "gy")
    row_share = rows_here // lax.axis_size("gy")
    mode_one = lax.dynamic_slice_in_dim(whole_rows, lax.axis_index("gy") * row_share, row_share, 0)
    mode_two = lax.psum(second_part, "gx")
    mode_three = lax.psum(hour_part, ("gx", "gy"))
    own_rows = core_side // lax.axis_size("gx")
    summed_rows = lax.psum_scatter(
        jnp.dot(core_first, flat_field, preferred_element_type=jnp.float32),
        "gx",
        scatter_dimension=0,
        tiled=True,
    )
    first_mode = summed_rows.astype(jnp.bfloat16).reshape(own_rows, cols_here, hour_count)
    spread_hours = lax.all_to_all(first_mode, "gy", split_axis=2, concat_axis=1, tiled=True)
    full_second = lax.all_gather(core_second, "gy", axis=1, tiled=True)
    mixed_rows = jnp.einsum(
        "bj,ajt->bat", full_second, spread_hours, preferred_element_type=jnp.float32
    ).astype(jnp.bfloat16)
    second_mode = lax.all_to_all(mixed_rows, "gy", split_axis=0, concat_axis=2, tiled=True)
    core_sketch = jnp.einsum(
        "bat,ct->abc", second_mode, core_hours, preferred_element_type=jnp.float32
    )
    return (mode_one, mode_two, mode_three, core_sketch)


def solution(mesh):
    in_specs = (
        P("gx", "gy", None),
        P("gy", None),
        P(),
        P("gx", None),
        P(),
        P("gx", None),
        P("gy", None),
        P(None, "gx"),
        P(None, "gy"),
        P(),
    )
    out_specs = (P(("gx", "gy"), None), P("gy", None), P(), P("gx", "gy", None))
    return jax.shard_map(
        on_device, mesh=mesh, in_specs=in_specs, out_specs=out_specs, check_vma=False
    )
```

profile of v0, /device:TPU:1, one launch (start us, length us, event | category | flops | bytes accessed | tf_op | source)
XLA Modules:
  0.0 497.8 jit_solution(17556011770635523015)
XLA Ops:
  7.3 0.9 copy-done
  8.2 1.6 fusion.16
  9.7 83.6 %fusion = f32[56,1024]{1,0:T(8,128)} fusion(f32[800,1024]{1,0:T(8,128)S(1)} %fusion.16), kind=kCustom, calls=%all-reduce-scatter | all-reduce-scatter fusion | flops 917505 | bytes 3507200
  93.3 1.0 convert.1
  94.3 1.3 collective-permute-start
  95.6 0.9 slice
  96.6 6.0 %collective-permute-start.1 = (bf16[34,1024]{1,0:T(8,128)(2,1)S(1)}, bf16[34,1024]{1,0:T(8,128)(2,1)S(1)}, u32[]{:S(2)}, u32[]{:S(2)}) collective-permute-start(bf16[34,1024]{1,0:T(8,128)(2,1)S(1)} %slice), channel_id=1, source_target_pairs={{0,32},{16,48},{32,64},{48,80},{64,96},{80,112},{96,128},{112,144}... | collective-permute-start | bytes 208904
  102.6 2.0 convolution_bitcast_fusion.2
  104.7 1.3 copy.59
  106.0 11.3 %while.14 = (s32[]{:T(128)}, f32[64,400]{1,0:T(8,128)S(1)}, bf16[96,16,64]{2,1,0:T(8,128)(2,1)S(1)}, bf16[96,400]{1,0:T(8,128)(2,1)}, bf16[16,400]{1,0:T(8,128)(...) while((s32[]{:T(128)}, f32[64,400]{1,0:T(8,128)S(1)}, ...), condition=%wide.region_3.0_spmd.clone, body=%wide.region_2.0_spmd.clone.sunk | while | flops 6716807 | bytes 373149 | solution.py:47
  111.7 0.7 dynamic-slice_convert_fusion.3
  112.6 0.7 dynamic-slice_convert_fusion.3
  113.6 0.7 dynamic-slice_convert_fusion.3
  119.3 1.3 concatenate
  121.2 1.2 reshape.39
  122.4 8.6 %all-to-all-start = ((bf16[16,2,1600]{2,1,0:T(2,128)(2,1)}), bf16[16,2,1600]{2,1,0:T(2,128)(2,1)S(1)}, u32[]{:S(2)}, u32[]{:S(2)}) async-start(bf16[16,2,1600]{2,1,0:T(2,128)(2,1)} %reshape.39), calls=%async_computation | async-start | bytes 212992 | tf_op jit(solution)/shard_map/all_to_all | solution.py:63
  131.1 25.7 %all_gather.3 = bf16[800,256]{0,1:T(8,128)(2,1)S(1)} all-gather(bf16[800,16]{0,1:T(8,128)(2,1)S(1)} %copy-done.8), channel_id=1, replica_groups=mesh['gx'=16,'gy'=16] {'gy'}, dimensions={1}, use_global_device_ids=true | all-gather | bytes 435200 | tf_op jit(solution)/shard_map/all_gather | solution.py:64
  156.8 0.8 reshape.40
  157.9 1.3 copy.63
  159.2 1.8 reshape.41
  161.0 3.5 all-to-all-start.1
  164.5 1.3 fusion.10
  165.8 48.6 %psum.22 = f32[16,400]{1,0:T(8,128)} all-reduce(f32[16,400]{1,0:T(8,128)S(1)} %fusion.10), channel_id=1, replica_groups=mesh['gx'=16,'gy'=16] {'gx'}, use_global_device_ids=true, to_apply=%region_1.0 | all-reduce | flops 6400 | bytes 51200 | tf_op jit(solution)/shard_map/psum | solution.py:53
  214.4 27.5 %all-reduce.5.cloned.1.call-done = f32[96,400]{1,0:T(8,128)} async-done(((f32[96,400]{1,0:T(8,128)}), f32[96,400]{1,0:T(8,128)}) %all-reduce.5.cloned.1.call-update) | async-done | bytes 153616 | tf_op jit(solution)/shard_map/psum | solution.py:50
  242.0 1.4 constant_dynamic-slice_fusion
  243.4 0.9 reshape.42
  244.2 1.7 copy.70
  245.9 2.0 copy.65
  247.9 1.7 convolution_bitcast_fusion.1
  249.6 5.7 %copy.67 = f32[50,50,800]{2,1,0:T(8,128)} copy(f32[50,50,800]{2,0,1:T(8,128)S(1)} %convolution_bitcast_fusion.1) | data formatting | bytes 16000000
  255.3 234.1 %all-reduce.7.cloned.1.call-done = f32[64,400]{1,0:T(8,128)} async-done(((f32[64,400]{1,0:T(8,128)}), f32[64,400]{1,0:T(8,128)}) %all-reduce.7.cloned.1.call-update) | async-done | bytes 102416 | tf_op jit(solution)/shard_map/psum | solution.py:54
  489.4 1.6 copy.81
  (73 shorter events, 11.2 us)
Async XLA Ops:
  7.2 1.0 copy-start
  7.2 110.8 %copy-start.10 = (u32[256]{0:T(256)S(1)}, u32[256]{0:T(256)}, u32[]{:S(2)}) copy-start(u32[256]{0:T(256)} %constant.42) | copy-start | bytes 3076
  7.2 95.3 %copy-start.6 = (bf16[64,400]{1,0:T(8,128)(2,1)S(1)}, bf16[64,400]{1,0:T(8,128)(2,1)}, u32[]{:S(2)}) copy-start(bf16[64,400]{1,0:T(8,128)(2,1)} %param.14) | copy-start | bytes 153604
  7.2 95.4 %copy-start.9 = (bf16[16,400]{1,0:T(8,128)(2,1)S(1)}, bf16[16,400]{1,0:T(8,128)(2,1)}, u32[]{:S(2)}) copy-start(bf16[16,400]{1,0:T(8,128)(2,1)} %param.13) | copy-start | bytes 38404
  7.2 98.8 %copy-start.3 = (bf16[16,400]{1,0:T(8,128)(2,1)S(1)}, bf16[16,400]{1,0:T(8,128)(2,1)}, u32[]{:S(2)}) copy-start(bf16[16,400]{1,0:T(8,128)(2,1)} %param.18) | copy-start | bytes 38404
  7.2 234.8 %all-reduce.5.cloned.1.call-start = ((), (), s32[]{:S(2)}) async-start(), calls=%async_computation.2 | async-start | bytes 393216 | tf_op jit(solution)/shard_map/psum | solution.py:50
  93.3 37.7 %copy-start.8 = (bf16[800,16]{0,1:T(8,128)(2,1)S(1)}, bf16[800,16]{0,1:T(8,128)(2,1)}, u32[]{:S(2)}) copy-start(bf16[800,16]{0,1:T(8,128)(2,1)} %param.20) | copy-start | bytes 76804
  93.3 63.4 %copy-start.5 = (bf16[96,400]{1,0:T(8,128)(2,1)S(1)}, bf16[96,400]{1,0:T(8,128)(2,1)}, u32[]{:S(2)}) copy-start(bf16[96,400]{1,0:T(8,128)(2,1)} %param.15) | copy-start | bytes 230404
  93.3 63.4 %copy-start.7 = (bf16[64,400]{1,0:T(8,128)(2,1)S(1)}, bf16[64,400]{1,0:T(8,128)(2,1)}, u32[]{:S(2)}) copy-start(bf16[64,400]{1,0:T(8,128)(2,1)} %param.16) | copy-start | bytes 153604
  94.3 25.0 %collective-permute-start = (bf16[56,1024]{1,0:T(8,128)(2,1)S(1)}, bf16[56,1024]{1,0:T(8,128)(2,1)S(1)}, u32[]{:S(2)}, u32[]{:S(2)}) collective-permute-start(bf16[56,1024]{1,0:T(8,128)(2,1)S(1)} %convert.1), channel_id=1, source_target_pairs={{0,16},{16,32},{32,48},{48,64},{64,80},{80,96},{96,112},{112,128},... | collective-permute-start | bytes 344072
  96.6 22.7 %collective-permute-start.1 = (bf16[34,1024]{1,0:T(8,128)(2,1)S(1)}, bf16[34,1024]{1,0:T(8,128)(2,1)S(1)}, u32[]{:S(2)}, u32[]{:S(2)}) collective-permute-start(bf16[34,1024]{1,0:T(8,128)(2,1)S(1)} %slice), channel_id=1, source_target_pairs={{0,32},{16,48},{32,64},{48,80},{64,96},{80,112},{96,128},{112,144}... | collective-permute-start | bytes 208904
  102.6 61.9 %copy-start.2 = (bf16[96,16,64]{0,2,1:T(8,128)(2,1)S(1)}, bf16[96,16,64]{0,2,1:T(8,128)(2,1)}, u32[]{:S(2)}) copy-start(bf16[96,16,64]{0,2,1:T(8,128)(2,1)} %param.12) | copy-start | bytes 589828
  104.7 384.7 %all-reduce.7.cloned.1.call-start = ((), (), s32[]{:S(2)}) async-start(), calls=%async_computation.3 | async-start | bytes 262144 | tf_op jit(solution)/shard_map/psum | solution.py:54
  117.3 0.7 copy-start.1
  122.4 34.4 %all-to-all-start = ((bf16[16,2,1600]{2,1,0:T(2,128)(2,1)}), bf16[16,2,1600]{2,1,0:T(2,128)(2,1)S(1)}, u32[]{:S(2)}, u32[]{:S(2)}) async-start(bf16[16,2,1600]{2,1,0:T(2,128)(2,1)} %reshape.39), calls=%async_computation | async-start | bytes 212992 | tf_op jit(solution)/shard_map/all_to_all | solution.py:63
  159.2 88.7 %copy-start.4 = (bf16[800,64]{0,1:T(8,128)(2,1)S(1)}, bf16[800,64]{0,1:T(8,128)(2,1)}, u32[]{:S(2)}) copy-start(bf16[800,64]{0,1:T(8,128)(2,1)} %param.21) | copy-start | bytes 307204
  161.0 82.3 %all-to-all-start.1 = ((bf16[16,2,5000]{2,1,0:T(2,128)(2,1)}), bf16[16,2,5000]{2,1,0:T(2,128)(2,1)S(1)}, u32[]{:S(2)}, u32[]{:S(2)}) async-start(bf16[16,2,5000]{2,1,0:T(2,128)(2,1)} %reshape.41), calls=%async_computation.1 | async-start | bytes 655360 | tf_op jit(solution)/shard_map/all_to_all | solution.py:68
Sparse Core Ops, SparseCore 0:
  104.8 137.1 all-reduce.4
  249.0 240.3 all-reduce.6
where the time goes:
time: 499 us; the launch traced here: 498 us
  waiting for transfers between devices  262 us (53%)
  blocking collectives  158 us (32%)
  local copies, waits for them, and re-layouts  24.5 us (5%)
  starting transfers between devices  19.5 us (4%)
  between operations  15 us (3%)
  other arithmetic  9.54 us (2%)
  matrix products  9.34 us (2%)
    psum x1, waiting for transfers between devices, on_device(): mode_three = lax.psum(hour_part, ('gx', 'gy'))  234 us
    unnamed x1, blocking collectives  83.6 us
    psum x1, blocking collectives, on_device(): mode_two = lax.psum(second_part, 'gx')  48.6 us
    psum x1, waiting for transfers between devices, on_device(): whole_rows = lax.psum(first_part, 'gy')  27.5 us
    all_gather x1, blocking collectives, on_device(): full_second = lax.all_gather(core_second, 'gy', axis=1, tiled=True)  25.7 us
    unnamed x32, local copies, waits for them, and re-layouts  17.6 us
  transfers between devices with their start and end apart: 6, of which 2 were waited for; matrix products, arithmetic and copies ran while one was open for 8% of the time, Pallas kernels for 0%

commit v1 on v0

v1 whole, which is shorter than its diff:
```python
import jax
import jax.numpy as jnp
from jax import lax
from jax.experimental import pallas as pl
from jax.experimental.pallas import tpu as pltpu
from jax.sharding import PartitionSpec as P

MESH = pl.DeviceIdType.MESH
F32 = jnp.float32
BF16 = jnp.bfloat16
N = 16
NZ = 8
WIN = 512
BLK = 64
OFFSETS = (0, -1, 1, -2, 2, -3, 3, -4)


def exchange_kernel(
    f_ref, cf_ref, c2_ref, s1_ref, h1_ref, f2_ref, h2_ref, f3_ref, s3_ref,
    rr_out, m1_out, m23_out,
    f32s, fblk, fall, cfall, c2f, c2all, s1f, s3f, acc, acct, fms, fmr, lhsf, sms, rr,
    m1a, m2a, m3a, m1s, m1r, g1s, g1r, g2s, g2r, g3s, g3r,
    fs, fr, ffs, ffr, zs, zr, ys, yr, cs, cr, p2s, p2r, p3s, p3r,
    m1ss, m1rs, g1ss, g1rs, g2ss, g2rs, g3ss, g3rs,
):
    mx, my = lax.axis_index("gx"), lax.axis_index("gy")
    core = lax.rem(my, 2)
    place = my // 2
    ylo, z = lax.rem(mx, 2), mx // 2
    yhi, x = lax.rem(place, 2), place // 2
    other = (mx, my + 1 - 2 * core)
    y = 2 * yhi + ylo

    def at_y(there):
        there = lax.rem(there, 4)
        return (2 * z + lax.rem(there, 2), 4 * x + 2 * (there // 2) + core)

    y_up, y_down = at_y(y + 1), at_y(y + 3)
    z_up = (2 * lax.rem(z + 1, NZ) + ylo, my)
    z_down = (2 * lax.rem(z + NZ - 1, NZ) + ylo, my)

    def send(src, dst, send_sem, recv_sem, device):
        return pltpu.make_async_remote_copy(
            src_ref=src, dst_ref=dst, send_sem=send_sem, recv_sem=recv_sem,
            device_id=device, device_id_type=MESH,
        )

    def gx_peer(r):
        return lax.rem(mx + r, N)

    def gy_peer(r):
        return lax.rem(my + r, N)

    def each(low, high, body):
        def step(i, carry):
            body(i)
            return carry

        lax.fori_loop(low, high, step, 0)

    barrier = pltpu.get_barrier_semaphore()

    def greet(r):
        pl.semaphore_signal(barrier, inc=1, device_id=(gx_peer(r), my), device_id_type=MESH)
        pl.semaphore_signal(barrier, inc=1, device_id=(mx, gy_peer(r)), device_id_type=MESH)

    each(1, N, greet)
    across = (mx + 1 - 2 * ylo, my + 2 - 4 * yhi)
    pl.semaphore_signal(barrier, inc=1, device_id=across, device_id_type=MESH)
    half = mx // 8
    same = jnp.logical_and(mx == my, half == core)

    def greet_turned(s):
        @pl.when(jnp.logical_not(jnp.logical_and(my == mx, 2 * s + half == my)))
        def _():
            pl.semaphore_signal(
                barrier, inc=1, device_id=(my, 2 * s + half), device_id_type=MESH
            )

    each(0, 8, greet_turned)

    for j in range(16):
        f32s[64 * j : 64 * j + 64, 0:96] = f_ref[j].astype(F32)
    for t in range(64):
        fblk[t // 4, t % 4] = f32s[pl.ds(t, 16, stride=64), :][:, 0:96].astype(BF16)

    cfall[mx, :, 384:512] = jnp.zeros((96, 128), BF16)

    @pl.when(core == 0)
    def _():
        cfall[mx] = cf_ref[:, 0:512]

    @pl.when(core == 1)
    def _():
        cfall[mx, :, 0:416] = cf_ref[:, 384:800]

    c2f[...] = jnp.zeros_like(c2f)
    for g in range(N):
        c2f[:, BLK * g : BLK * g + 50] = c2_ref[:, 50 * g : 50 * g + 50].astype(F32)
    c2all[place, core] = c2f[...].astype(BF16)

    pl.semaphore_wait(barrier, 2 * (N - 1) + 1 + 8 - same.astype(jnp.int32))

    def shard(o, low):
        return 2 * lax.rem(z + o + NZ, NZ) + low

    def z_copy(direction, step):
        o = -direction * (step - 1)
        index = step - 1 if direction > 0 else 3 + step
        slot = cfall.at[shard(o, ylo)]
        return send(slot, slot, zs.at[index], zr.at[index], z_up if direction > 0 else z_down)

    def y_copy(o, h):
        slot = cfall.at[shard(o, ylo), pl.ds(48 * h, 48)]
        index = 2 * (o + 4) + h
        return send(slot, slot, ys.at[index], yr.at[index], y_up if h == 0 else y_down)

    def pass_on(o):
        y_copy(o, 0).start()
        y_copy(o, 1).start()

    def ring(step):
        z_copy(1, step).wait_recv()
        if step < 4:
            z_copy(1, step + 1).start()
        if step < 4:
            z_copy(-1, step).wait_recv()
            if step < 3:
                z_copy(-1, step + 1).start()
        pass_on(-step)
        if step < 4:
            pass_on(step)

    def f_copy(r):
        return send(
            fblk.at[gx_peer(r)], fall.at[mx, :, core], fs.at[r], fr.at[r], (gx_peer(r), my)
        )

    def f_forward(r):
        slot = fall.at[lax.rem(mx + N - r, N), :, core]
        return send(slot, slot, ffs.at[r], ffr.at[r], other)

    z_copy(1, 1).start()
    z_copy(-1, 1).start()
    pass_on(0)
    each(1, N, lambda r: f_copy(r).start())
    for t in range(4):
        fall[mx, t, core] = fblk[mx, t]
    f_forward(0).start()

    c2_y = send(
        c2all.at[place, core], c2all.at[place, core], cs.at[0], cr.at[0],
        (mx, my + 2 - 4 * yhi),
    )
    c2_y.start()

    def c2_x(r):
        pair = c2all.at[pl.ds(2 * x, 2), core]
        return send(
            pair, pair, cs.at[r], cr.at[r], (mx, 4 * lax.rem(x + r, 4) + 2 * yhi + core)
        )

    mine = c2all.at[:, core]
    c2_core = send(mine, mine, cs.at[4], cr.at[4], other)

    s1f[...] = s1_ref[...].astype(F32)
    s3f[...] = s3_ref[...].astype(F32)
    m1a[...] = jnp.zeros_like(m1a)
    m3a[...] = jnp.zeros_like(m3a)
    m1s[...] = jnp.zeros_like(m1s)
    g1s[...] = jnp.zeros_like(g1s)

    def modes(low, high):
        def one(j):
            rows = f_ref[j]
            turned = (((0,), (0,)), ((), ()))
            by_one = lax.dot_general(rows, h1_ref[...], turned, preferred_element_type=F32)
            m1a[...] += by_one * s1f[pl.ds(j, 1), :]
            by_two = lax.dot_general(rows, h2_ref[...], turned, preferred_element_type=F32)
            m2a[pl.ds(j, 1), :] = jnp.sum(by_two * f2_ref[...].astype(F32), axis=0, keepdims=True)
            by_three = jnp.dot(rows, f3_ref[...], preferred_element_type=F32)
            m3a[...] += by_three * s3f[pl.ds(j, 1), :]

        each(low, high, one)

    modes(0, 5)
    ring(1)
    modes(5, 10)
    c2_y.wait_recv()
    each(1, 4, lambda r: c2_x(r).start())
    ring(2)
    modes(10, 16)
    ring(3)

    def field_arrives(r):
        f_copy(r).wait_recv()
        f_forward(r).start()

    each(1, N, field_arrives)
    ring(4)

    for g in range(N):
        g1s[g, 0:4] = m3a[4 * g : 4 * g + 4]
        g1s[g, 4:5] = m2a[g : g + 1]
        m1s[g, 0:6] = m1a[6 * g : 6 * g + 6]

    def g1_copy(r):
        return send(g1s.at[gx_peer(r)], g1r.at[mx], g1ss.at[r], g1rs.at[r], (gx_peer(r), my))

    def m1_copy(r):
        return send(m1s.at[gy_peer(r)], m1r.at[my], m1ss.at[r], m1rs.at[r], (mx, gy_peer(r)))

    def g2_copy(r):
        return send(g2s, g2r.at[my], g2ss.at[r], g2rs.at[r], (mx, gy_peer(r)))

    def g3_copy(r):
        return send(g3s, g3r.at[mx], g3ss.at[r], g3rs.at[r], (gx_peer(r), my))

    each(1, N, lambda r: g1_copy(r).start())
    g1r[mx] = g1s[mx]
    m1r[my] = m1s[my]

    each(1, 4, lambda r: c2_x(r).wait_recv())
    c2_core.start()
    each(0, N, lambda r: f_forward(r).wait_recv())

    def add_shard(g):
        acc[...] += jnp.dot(fall[g].reshape(128, 96), cfall[g], preferred_element_type=F32)

    acc[...] = jnp.zeros_like(acc)
    for o in OFFSETS:
        add_shard(shard(o, ylo))
        y_copy(o, 0).wait_recv()
        y_copy(o, 1).wait_recv()
        add_shard(shard(o, 1 - ylo))
    acct[...] = acc[...].T

    def m_copy(m):
        return send(fms.at[m], fmr.at[place], p2s.at[m], p2r.at[place], (8 * core + m, mx))

    def not_self(m):
        return jnp.logical_not(jnp.logical_and(8 * core + m == mx, mx == my))

    for m in range(8):
        fms[m] = acct[pl.ds(16 * core + 50 * m, BLK), :].astype(BF16)

        @pl.when(not_self(m))
        def _():
            m_copy(m).start()

        @pl.when(jnp.logical_not(not_self(m)))
        def _():
            fmr[place] = fms[m]

    each(1, N, lambda r: m1_copy(r).start())

    each(1, N, lambda r: g1_copy(r).wait_recv())
    g2s[...] = jnp.sum(g1r[...], axis=0)
    each(1, N, lambda r: g2_copy(r).start())
    g2r[my] = g2s[...]

    c2_core.wait_recv()

    def first_arrives(s):
        @pl.when(jnp.logical_not(jnp.logical_and(my == mx, 2 * s + half == my)))
        def _():
            send(fms.at[0], fmr.at[s], p2s.at[0], p2r.at[s], other).wait_recv()

    each(0, 8, first_arrives)
    for s in range(8):
        part = fmr[s].astype(F32)
        for t in range(4):
            lhsf[BLK * t : BLK * t + BLK, 32 * s : 32 * s + 32] = part[:, 32 * t : 32 * t + 32]
    lhs = lhsf[...].astype(BF16)
    low_lanes = lax.broadcasted_iota(jnp.int32, (BLK, 128), 1) < BLK
    for u in range(4):
        rhs = c2all[:, :, :, 256 * u : 256 * u + 256].reshape(256, 256)
        got = jnp.dot(lhs, rhs, preferred_element_type=F32)
        for v in range(2):
            for p in range(2):
                first = got[2 * BLK * p : 2 * BLK * p + BLK, 128 * v : 128 * v + 128]
                second = got[2 * BLK * p + BLK : 2 * BLK * p + 2 * BLK, 128 * v : 128 * v + 128]
                g = 4 * u + 2 * v
                sms[g, p] = jnp.where(low_lanes, first, pltpu.roll(second, BLK, 1)).astype(BF16)
                sms[g + 1, p] = jnp.where(low_lanes, pltpu.roll(first, BLK, 1), second).astype(BF16)

    def p3_copy(r):
        return send(
            sms.at[gy_peer(r)], rr.at[pl.ds(2 * my, 2)], p3s.at[r], p3r.at[r], (mx, gy_peer(r))
        )

    each(1, N, lambda r: p3_copy(r).start())
    rr[pl.ds(2 * my, 2)] = sms[my]

    each(1, N, lambda r: g2_copy(r).wait_recv())
    g3s[...] = jnp.sum(g2r[...], axis=0)
    g3s[4:5] = g2s[4:5]
    each(1, N, lambda r: g3_copy(r).start())
    g3r[mx] = g3s[...]

    each(1, N, lambda r: m1_copy(r).wait_recv())
    m1_out[...] = jnp.sum(m1r[...], axis=0)
    each(1, N, lambda r: g3_copy(r).wait_recv())
    m23_out[...] = g3r[...]
    each(1, N, lambda r: p3_copy(r).wait_recv())
    rr_out[...] = rr[...]

    for step in range(1, 5):
        z_copy(1, step).wait_send()
    for step in range(1, 4):
        z_copy(-1, step).wait_send()
    for o in OFFSETS:
        y_copy(o, 0).wait_send()
        y_copy(o, 1).wait_send()
    c2_y.wait_send()
    each(1, 4, lambda r: c2_x(r).wait_send())
    c2_core.wait_send()
    f_forward(0).wait_send()

    def left(r):
        f_copy(r).wait_send()
        f_forward(r).wait_send()
        g1_copy(r).wait_send()
        m1_copy(r).wait_send()
        g2_copy(r).wait_send()
        g3_copy(r).wait_send()
        p3_copy(r).wait_send()

    each(1, N, left)
    for m in range(8):

        @pl.when(not_self(m))
        def _():
            m_copy(m).wait_send()


CHUNK = 10


def hours_kernel(rr_ref, c3_ref, m1_ref, m23_ref, core_out, one_out, two_out, three_out, rrf, c3b, lhs):
    step = pl.program_id(0)

    @pl.when(step == 0)
    def _():
        for r in range(32):
            rrf[BLK * r : BLK * r + BLK, :] = rr_ref[r].astype(F32)
        row = lax.broadcasted_iota(jnp.int32, (64, 64), 0)
        hour = lax.broadcasted_iota(jnp.int32, (64, 64), 1)
        evens_first = hour == jnp.where(row < 32, 2 * row, 2 * row - 63)
        c3b[...] = jnp.dot(
            evens_first.astype(BF16), c3_ref[...], preferred_element_type=F32
        ).astype(BF16)
        one_out[...] = m1_ref[0:6, :]
        for g in range(N):
            three_out[4 * g : 4 * g + 4, :] = m23_ref[g, 0:4]
            two_out[g : g + 1, :] = m23_ref[g, 4:5]

    for k in range(CHUNK):
        turned = rrf[pl.ds(step * CHUNK + k, 32, stride=BLK), :].T
        lhs[56 * k : 56 * k + 56, 0:32] = turned[0:56]
        lhs[56 * k : 56 * k + 56, 32:64] = turned[BLK : BLK + 56]
    got = jnp.dot(lhs[...].astype(BF16), c3b[...], preferred_element_type=F32)
    for k in range(CHUNK):
        core_out[k] = got[56 * k : 56 * k + 50]


def on_device(
    field_slab, one_by_second, one_by_hours, two_by_first, two_by_hours,
    three_by_first, three_by_second, core_first, core_second, core_hours,
):
    vmem = pl.BlockSpec(memory_space=pltpu.VMEM)
    dma = pltpu.SemaphoreType.DMA
    rr, m1, m23 = pl.pallas_call(
        exchange_kernel,
        out_shape=(
            jax.ShapeDtypeStruct((32, BLK, 128), BF16),
            jax.ShapeDtypeStruct((8, 400), F32),
            jax.ShapeDtypeStruct((N, 8, 400), F32),
        ),
        in_specs=[vmem] * 9,
        out_specs=(vmem, vmem, vmem),
        scratch_shapes=[
            pltpu.VMEM((1024, 128), F32),
            pltpu.VMEM((N, 4, 16, 96), BF16),
            pltpu.VMEM((N, 4, 2, 16, 96), BF16),
            pltpu.VMEM((N, 96, WIN), BF16),
            pltpu.VMEM((16, 1024), F32),
            pltpu.VMEM((8, 2, 16, 1024), BF16),
            pltpu.VMEM((16, 400), F32),
            pltpu.VMEM((16, 400), F32),
            pltpu.VMEM((128, WIN), F32),
            pltpu.VMEM((WIN, 128), F32),
            pltpu.VMEM((8, BLK, 128), BF16),
            pltpu.VMEM((8, BLK, 128), BF16),
            pltpu.VMEM((256, 256), F32),
            pltpu.VMEM((N, 2, BLK, 128), BF16),
            pltpu.VMEM((32, BLK, 128), BF16),
            pltpu.VMEM((96, 400), F32),
            pltpu.VMEM((16, 400), F32),
            pltpu.VMEM((64, 400), F32),
            pltpu.VMEM((N, 8, 400), F32),
            pltpu.VMEM((N, 8, 400), F32),
            pltpu.VMEM((N, 8, 400), F32),
            pltpu.VMEM((N, 8, 400), F32),
            pltpu.VMEM((8, 400), F32),
            pltpu.VMEM((N, 8, 400), F32),
            pltpu.VMEM((8, 400), F32),
            pltpu.VMEM((N, 8, 400), F32),
            dma((N,)), dma((N,)), dma((N,)), dma((N,)),
            dma((7,)), dma((7,)), dma((16,)), dma((16,)),
            dma((5,)), dma((5,)), dma((8,)), dma((8,)), dma((N,)), dma((N,)),
            dma((N,)), dma((N,)), dma((N,)), dma((N,)), dma((N,)), dma((N,)), dma((N,)), dma((N,)),
        ],
        compiler_params=pltpu.CompilerParams(
            collective_id=0, has_side_effects=True, vmem_limit_bytes=32 * 2**20
        ),
        cost_estimate=pl.CostEstimate(flops=500_000_000, bytes_accessed=2_000_000, transcendentals=0),
        name="exchange",
    )(
        jnp.transpose(field_slab, (1, 2, 0)), core_first.T, core_second.T,
        one_by_second, one_by_hours, two_by_first, two_by_hours, three_by_first, three_by_second,
    )

    def whole(shape):
        return pl.BlockSpec(shape, lambda step: (0,) * len(shape))

    core_sketch, mode_one, mode_two, mode_three = pl.pallas_call(
        hours_kernel,
        grid=(50 // CHUNK,),
        out_shape=(
            jax.ShapeDtypeStruct((50, 50, 800), F32),
            jax.ShapeDtypeStruct((6, 400), F32),
            jax.ShapeDtypeStruct((16, 400), F32),
            jax.ShapeDtypeStruct((64, 400), F32),
        ),
        in_specs=[whole((32, BLK, 128)), whole((64, 800)), whole((8, 400)), whole((N, 8, 400))],
        out_specs=(
            pl.BlockSpec((CHUNK, 50, 800), lambda step: (step, 0, 0)),
            whole((6, 400)), whole((16, 400)), whole((64, 400)),
        ),
        scratch_shapes=[
            pltpu.VMEM((32 * BLK, 128), F32),
            pltpu.VMEM((64, 800), BF16),
            pltpu.VMEM((56 * CHUNK, 64), F32),
        ],
        compiler_params=pltpu.CompilerParams(vmem_limit_bytes=32 * 2**20),
        cost_estimate=pl.CostEstimate(flops=260_000_000, bytes_accessed=11_000_000, transcendentals=0),
        name="hours",
    )(rr, core_hours.T, m1, m23)
    return mode_one, mode_two, mode_three, core_sketch


def solution(mesh):
    in_specs = (
        P("gx", "gy", None),
        P("gy", None),
        P(),
        P("gx", None),
        P(),
        P("gx", None),
        P("gy", None),
        P(None, "gx"),
        P(None, "gy"),
        P(),
    )
    out_specs = (P(("gx", "gy"), None), P("gy", None), P(), P("gx", "gy", None))
    return jax.shard_map(
        on_device, mesh=mesh, in_specs=in_specs, out_specs=out_specs, check_vma=False
    )
```

time: 499 us -> 75.9 us (0.15)
  waiting for transfers between devices: 262 us -> 0 us
  blocking collectives: 158 us -> 0 us
  Pallas kernels: 0 us -> 66.1 us
  starting transfers between devices: 19.5 us -> 0 us
  local copies, waits for them, and re-layouts: 24.5 us -> 8.4 us
  between operations: 15 us -> 0.67 us
  other arithmetic: 9.54 us -> 0 us
  matrix products: 9.34 us -> 0 us
    psum x2 -> x0, waiting for transfers between devices: 262 us -> none  [the longest x1 234 us: on_device(): mode_three = lax.psum(hour_part, ('gx', 'gy'))]
    unnamed x1 -> x0, blocking collectives: 83.6 us -> none
    pallas_call x0 -> x2, Pallas kernels: none -> 66.1 us  [the longest x1 59.8 us: on_device(): pl.pallas_call(exchange_kernel, out_shape=(jax.ShapeDtypeStruct((32, BLK,...]
    psum x1 -> x0, blocking collectives: 48.6 us -> none  [on_device(): mode_two = lax.psum(second_part, 'gx')]
    all_gather x1 -> x0, blocking collectives: 25.7 us -> none  [on_device(): full_second = lax.all_gather(core_second, 'gy', axis=1, tiled=True)]
    all_to_all x2 -> x0, starting transfers between devices: 12.1 us -> none  [the longest x1 8.63 us: on_device(): lax.all_to_all(first_mode, 'gy', split_axis=2, concat_axis=1, tiled=True)]
    dot_general x17 -> x0, matrix products: 9.34 us -> none  [the longest x12 2.47 us: hour_block(): lax.dot_general(row_block, test_three, (((0,), (0,)), ((), ())), preferre...]
    unnamed x32 -> x20, local copies, waits for them, and re-layouts: 17.6 us -> 8.4 us
  transfers between devices with their start and end apart: 6 -> 0, of which waited for: 2 -> 0; matrix products, arithmetic and copies ran while one was open for 8% -> 0% of each run, Pallas kernels for 0% -> 0%
where the time goes in v1:
time: 75.9 us; the launch traced here: 75.2 us
  Pallas kernels  66.1 us (87%)
  local copies, waits for them, and re-layouts  8.4 us (11%)
    pallas_call x1, Pallas kernels, on_device(): pl.pallas_call(exchange_kernel, out_shape=(jax.ShapeDtypeStruct((32, BLK,...  59.8 us
    unnamed x20, local copies, waits for them, and re-layouts  8.4 us
    pallas_call x1, Pallas kernels, on_device(): pl.pallas_call(hours_kernel, grid=(50 // CHUNK,), out_shape=(jax.ShapeDty...  6.3 us

profile of v1, /device:TPU:1, one launch (start us, length us, event | category | flops | bytes accessed | tf_op | source)
XLA Modules:
  0.0 75.2 jit_solution(9595465894804074822)
XLA Ops:
  0.6 0.0 copy-start
  0.6 0.9 %copy-done = bf16[96,16,64]{0,2,1:T(8,128)(2,1)S(1)} copy-done((bf16[96,16,64]{0,2,1:T(8,128)(2,1)S(1)}, bf16[96,16,64]{0,2,1:T(8,128)(2,1)}, u32[]{:S(2)}) %copy-start) | copy-done | bytes 196632
  1.6 0.0 copy-start.1
  1.6 0.9 %copy-done.1 = bf16[800,96]{0,1:T(8,128)(2,1)S(1)} copy-done((bf16[800,96]{0,1:T(8,128)(2,1)S(1)}, bf16[800,96]{0,1:T(8,128)(2,1)}, u32[]{:S(2)}) %copy-start.1) | copy-done | bytes 153624
  2.5 0.0 copy-start.3
  2.5 0.9 %copy-done.3 = bf16[96,400]{1,0:T(8,128)(2,1)S(1)} copy-done((bf16[96,400]{1,0:T(8,128)(2,1)S(1)}, bf16[96,400]{1,0:T(8,128)(2,1)}, u32[]{:S(2)}) %copy-start.3) | copy-done | bytes 76824
  3.4 0.0 copy-start.4
  3.4 0.9 %copy-done.4 = bf16[96,400]{1,0:T(8,128)(2,1)S(1)} copy-done((bf16[96,400]{1,0:T(8,128)(2,1)S(1)}, bf16[96,400]{1,0:T(8,128)(2,1)}, u32[]{:S(2)}) %copy-start.4) | copy-done | bytes 76824
  4.3 0.0 copy-start.5
  4.3 0.8 %copy-done.5 = bf16[64,400]{1,0:T(8,128)(2,1)S(1)} copy-done((bf16[64,400]{1,0:T(8,128)(2,1)S(1)}, bf16[64,400]{1,0:T(8,128)(2,1)}, u32[]{:S(2)}) %copy-start.5) | copy-done | bytes 51224
  5.1 0.0 copy-start.6
  5.1 0.8 %copy-done.6 = bf16[64,400]{1,0:T(8,128)(2,1)S(1)} copy-done((bf16[64,400]{1,0:T(8,128)(2,1)S(1)}, bf16[64,400]{1,0:T(8,128)(2,1)}, u32[]{:S(2)}) %copy-start.6) | copy-done | bytes 51224
  6.0 0.0 copy-start.7
  6.0 0.7 copy-done.7
  6.7 0.0 copy-start.8
  6.7 0.7 copy-done.8
  7.4 0.0 copy-start.9
  7.4 0.7 copy-done.9
  8.2 59.8 %exchange.1 = (bf16[32,64,128]{2,1,0:T(8,128)(2,1)S(1)}, f32[8,400]{1,0:T(8,128)S(1)}, f32[16,8,400]{2,1,0:T(8,128)S(1)}) custom-call(bf16[16,64,96]{2,1,0:T(8,128)(2,1)S(1)} %bitcast.4, bf16[96,800]{1,0:T(8,128)(2,1)S(1)} %bitcast.5, bf16[16,800]{1,0:T(8,128)(2,1)S(1)} %bitcast.7, bf16[16,400]{1,0:T(8,128)(2,1)S(1)} %copy-done.8, ...), custom_call_target="tpu_custom_call" | custom-call | flops 500000000 | bytes 2000000 | tf_op jit(solution)/shard_map/exchange/pallas_call | solution.py:373
  68.0 0.0 copy-start.2
  68.0 0.9 %copy-done.2 = bf16[800,64]{0,1:T(8,128)(2,1)S(1)} copy-done((bf16[800,64]{0,1:T(8,128)(2,1)S(1)}, bf16[800,64]{0,1:T(8,128)(2,1)}, u32[]{:S(2)}) %copy-start.2) | copy-done | bytes 102424
  68.9 6.3 %hours.1 = (f32[50,50,800]{2,1,0:T(8,128)}, f32[6,400]{1,0:T(8,128)}, f32[16,400]{1,0:T(8,128)}, f32[64,400]{1,0:T(8,128)}) custom-call(bf16[32,64,128]{2,1,0:T(8,128)(2,1)S(1)} %get-tuple-element.11.rr_ref, bf16[64,800]{1,0:T(8,128)(2,1)S(1)} %bitcast.6, f32[8,400]{1,0:T(8,128)S(1)} %get-tuple-element.12.m1_ref, f32[16,8,400]{2,1,0:T(8,128)S(1)} %get-tuple-element.13.m23_ref), custom_call_target="tpu_custom_call" | custom-call | flops 260000000 | bytes 11000000 | tf_op jit(solution)/shard_map/hours/pallas_call | solution.py:427
Async XLA Ops:
  0.6 1.0 %copy-start = (bf16[96,16,64]{0,2,1:T(8,128)(2,1)S(1)}, bf16[96,16,64]{0,2,1:T(8,128)(2,1)}, u32[]{:S(2)}) copy-start(bf16[96,16,64]{0,2,1:T(8,128)(2,1)} %param.10) | copy-start | bytes 589828
  1.6 0.9 %copy-start.1 = (bf16[800,96]{0,1:T(8,128)(2,1)S(1)}, bf16[800,96]{0,1:T(8,128)(2,1)}, u32[]{:S(2)}) copy-start(bf16[800,96]{0,1:T(8,128)(2,1)} %param.17) | copy-start | bytes 460804
  2.5 0.9 %copy-start.3 = (bf16[96,400]{1,0:T(8,128)(2,1)S(1)}, bf16[96,400]{1,0:T(8,128)(2,1)}, u32[]{:S(2)}) copy-start(bf16[96,400]{1,0:T(8,128)(2,1)} %f2_ref.1) | copy-start | bytes 230404
  3.4 0.9 %copy-start.4 = (bf16[96,400]{1,0:T(8,128)(2,1)S(1)}, bf16[96,400]{1,0:T(8,128)(2,1)}, u32[]{:S(2)}) copy-start(bf16[96,400]{1,0:T(8,128)(2,1)} %f3_ref.1) | copy-start | bytes 230404
  4.3 0.8 %copy-start.5 = (bf16[64,400]{1,0:T(8,128)(2,1)S(1)}, bf16[64,400]{1,0:T(8,128)(2,1)}, u32[]{:S(2)}) copy-start(bf16[64,400]{1,0:T(8,128)(2,1)} %h1_ref.1) | copy-start | bytes 153604
  5.1 0.8 %copy-start.6 = (bf16[64,400]{1,0:T(8,128)(2,1)S(1)}, bf16[64,400]{1,0:T(8,128)(2,1)}, u32[]{:S(2)}) copy-start(bf16[64,400]{1,0:T(8,128)(2,1)} %h2_ref.1) | copy-start | bytes 153604
  6.0 0.7 copy-start.7
  6.7 0.7 copy-start.8
  7.4 0.7 copy-start.9
  68.0 0.9 %copy-start.2 = (bf16[800,64]{0,1:T(8,128)(2,1)S(1)}, bf16[800,64]{0,1:T(8,128)(2,1)}, u32[]{:S(2)}) copy-start(bf16[800,64]{0,1:T(8,128)(2,1)} %param.19) | copy-start | bytes 307204

commit v2 on v1

v2 whole, which is shorter than its diff:
```python
import jax
import jax.numpy as jnp
from jax import lax
from jax.experimental import pallas as pl
from jax.experimental.pallas import tpu as pltpu
from jax.sharding import PartitionSpec as P

MESH = pl.DeviceIdType.MESH
F32 = jnp.float32
BF16 = jnp.bfloat16
N = 16
NZ = 8
WIN = 256
BLK = 64
OFFSETS = (0, -1, 1, -2, 2, -3, 3, -4)


def exchange_kernel(
    f_hbm, cf_hbm, c2_hbm, c3_hbm, s1_hbm, h1_hbm, f2_hbm, h2_hbm, f3_hbm, s3_hbm,
    rr_out, c3_out, one_out, two_out, three_out,
    f_ref, cf_ref, c2_ref, c3_ref, s1_ref, h1_ref, f2_ref, h2_ref, f3_ref, s3_ref,
    f32s, fblk, fall, cfall, c2f, c2all, s1f, s3f, acc, acct, fms, fmr, lhsf, sms, rr,
    m1a, m2a, m3a, a1s, a1r, t2s, t2r, g2s, g2r, g3s, g3r,
    loads, fs, fr, fxs, fxr, fcs, fcr, zs, zr, ys, yr, cs, cr, p2s, p2r, p3s, p3r,
    a1ss, a1rs, t2ss, t2rs, g2ss, g2rs, g3ss, g3rs,
):
    mx, my = lax.axis_index("gx"), lax.axis_index("gy")
    ylo, z = lax.rem(mx, 2), mx // 2
    core, yhi, x = lax.rem(my, 2), lax.rem(my // 2, 2), my // 4
    xlo, xhi = lax.rem(x, 2), x // 2
    quarter, four = 2 * xlo + core, 2 * xhi + yhi
    other_core = (mx, my + 1 - 2 * core)
    other_x = (mx, my + 4 - 8 * xlo)
    y = 2 * yhi + ylo

    def at_y(there):
        there = lax.rem(there, 4)
        return (2 * z + lax.rem(there, 2), 4 * x + 2 * (there // 2) + core)

    y_up, y_down = at_y(y + 1), at_y(y + 3)
    z_up = (2 * lax.rem(z + 1, NZ) + ylo, my)
    z_down = (2 * lax.rem(z + NZ - 1, NZ) + ylo, my)

    def send(src, dst, send_sem, recv_sem, device):
        return pltpu.make_async_remote_copy(
            src_ref=src, dst_ref=dst, send_sem=send_sem, recv_sem=recv_sem,
            device_id=device, device_id_type=MESH,
        )

    def gx_peer(r):
        return lax.rem(mx + r, N)

    def gy_peer(r):
        return lax.rem(my + r, N)

    def each(low, high, body):
        def step(i, carry):
            body(i)
            return carry

        lax.fori_loop(low, high, step, 0)

    pairs = (
        (f_hbm, f_ref), (cf_hbm, cf_ref), (c2_hbm, c2_ref), (h1_hbm, h1_ref), (h2_hbm, h2_ref),
        (f2_hbm, f2_ref), (f3_hbm, f3_ref), (s1_hbm, s1_ref), (s3_hbm, s3_ref), (c3_hbm, c3_ref),
    )
    load = [pltpu.make_async_copy(src, dst, loads.at[i]) for i, (src, dst) in enumerate(pairs)]
    for one in load:
        one.start()

    barrier = pltpu.get_barrier_semaphore()

    def greet(r):
        pl.semaphore_signal(barrier, inc=1, device_id=(gx_peer(r), my), device_id_type=MESH)
        pl.semaphore_signal(barrier, inc=1, device_id=(mx, gy_peer(r)), device_id_type=MESH)

    each(1, N, greet)
    across = (mx + 1 - 2 * ylo, my + 2 - 4 * yhi)
    pl.semaphore_signal(barrier, inc=1, device_id=across, device_id_type=MESH)

    load[1].wait()
    cfall[mx, :, 128:256] = jnp.zeros((96, 128), BF16)
    for q in range(4):

        @pl.when(quarter == q)
        def _():
            cfall[mx, :, 0:200] = cf_ref[:, 200 * q : 200 * q + 200]

    load[0].wait()
    for j in range(16):
        f32s[64 * j : 64 * j + 64, 0:96] = f_ref[j].astype(F32)
    for t in range(64):
        fblk[t // 4, t % 4] = f32s[pl.ds(t, 16, stride=64), :][:, 0:96].astype(BF16)
    for t in range(4):
        fall[mx, t, quarter] = fblk[mx, t]

    pl.semaphore_wait(barrier, 2 * (N - 1) + 1)

    def shard(o, low):
        return 2 * lax.rem(z + o + NZ, NZ) + low

    def z_copy(direction, step):
        o = -direction * (step - 1)
        index = step - 1 if direction > 0 else 3 + step
        slot = cfall.at[shard(o, ylo)]
        return send(slot, slot, zs.at[index], zr.at[index], z_up if direction > 0 else z_down)

    def y_copy(o, h):
        slot = cfall.at[shard(o, ylo), pl.ds(48 * h, 48)]
        index = 2 * (o + 4) + h
        return send(slot, slot, ys.at[index], yr.at[index], y_up if h == 0 else y_down)

    def pass_on(o):
        y_copy(o, 0).start()
        y_copy(o, 1).start()

    def ring(step):
        z_copy(1, step).wait_recv()
        if step < 4:
            z_copy(1, step + 1).start()
            z_copy(-1, step).wait_recv()
            if step < 3:
                z_copy(-1, step + 1).start()
        pass_on(-step)
        if step < 4:
            pass_on(step)

    def f_copy(r):
        return send(
            fblk.at[gx_peer(r)], fall.at[mx, :, quarter], fs.at[r], fr.at[r], (gx_peer(r), my)
        )

    def f_x(r):
        slot = fall.at[lax.rem(mx + N - r, N), :, quarter]
        return send(slot, slot, fxs.at[r], fxr.at[r], other_x)

    own_columns = fall.at[:, :, quarter]
    f_core = send(own_columns, own_columns, fcs.at[0], fcr.at[0], other_core)
    x_columns = fall.at[:, :, quarter + 2 - 4 * xlo]
    f_x_core = send(x_columns, x_columns, fcs.at[1], fcr.at[1], other_core)

    z_copy(1, 1).start()
    z_copy(-1, 1).start()
    pass_on(0)
    each(1, N, lambda r: f_copy(r).start())
    f_x(0).start()

    for one in load[2:]:
        one.wait()
    s1f[...] = s1_ref[...].astype(F32)
    s3f[...] = s3_ref[...].astype(F32)
    m1a[...] = jnp.zeros_like(m1a)
    m3a[...] = jnp.zeros_like(m3a)

    def modes(low, high):
        def one(j):
            rows = f_ref[j]
            turned = (((0,), (0,)), ((), ()))
            by_one = lax.dot_general(rows, h1_ref[...], turned, preferred_element_type=F32)
            m1a[...] += by_one * s1f[pl.ds(j, 1), :]
            by_two = lax.dot_general(rows, h2_ref[...], turned, preferred_element_type=F32)
            m2a[pl.ds(j, 1), :] = jnp.sum(by_two * f2_ref[...].astype(F32), axis=0, keepdims=True)
            by_three = jnp.dot(rows, f3_ref[...], preferred_element_type=F32)
            m3a[...] += by_three * s3f[pl.ds(j, 1), :]

        each(low, high, one)

    modes(0, 8)
    ring(1)
    modes(8, 16)

    def a1_copy(r):
        return send(a1s.at[gy_peer(r)], a1r.at[my], a1ss.at[r], a1rs.at[r], (mx, gy_peer(r)))

    def t2_copy(r):
        return send(t2s.at[gx_peer(r)], t2r.at[mx], t2ss.at[r], t2rs.at[r], (gx_peer(r), my))

    def g2_copy(r):
        return send(g2s, g2r.at[mx], g2ss.at[r], g2rs.at[r], (gx_peer(r), my))

    def g3_copy(r):
        return send(g3s, g3r.at[my], g3ss.at[r], g3rs.at[r], (mx, gy_peer(r)))

    a1s[:, 1] = jnp.zeros((N, 4, 400), F32)
    for g in range(N):
        a1s[g, 0] = m1a[6 * g : 6 * g + 4]
        a1s[g, 1, 0:2] = m1a[6 * g + 4 : 6 * g + 6]
        a1s[g, 2] = m3a[4 * g : 4 * g + 4]
        t2s[g] = m2a[g : g + 1]

    def first_exchange(r):
        t2_copy(r).start()
        a1_copy(r).start()

    each(1, N, first_exchange)
    a1r[my] = a1s[my]
    t2r[mx] = t2s[mx]
    ring(2)

    c2f[...] = jnp.zeros_like(c2f)
    for g in range(N):
        c2f[:, BLK * g : BLK * g + 50] = c2_ref[:, 50 * g : 50 * g + 50].astype(F32)
    c2all[four, xlo, core] = c2f[...].astype(BF16)
    c2_own = c2all.at[four, xlo, core]
    c2_y = send(c2_own, c2_own, cs.at[0], cr.at[0], (mx, my + 2 - 4 * yhi))
    c2_y.start()

    def c2_x(r):
        pair = c2all.at[pl.ds(2 * xhi, 2), xlo, core]
        return send(
            pair, pair, cs.at[r], cr.at[r], (mx, 4 * lax.rem(x + r, 4) + 2 * yhi + core)
        )

    c2_mine = c2all.at[:, :, core]
    c2_core = send(c2_mine, c2_mine, cs.at[4], cr.at[4], other_core)

    def field_arrives(r):
        f_copy(r).wait_recv()
        f_x(r).start()

    each(1, N, field_arrives)
    f_core.start()
    ring(3)
    c2_y.wait_recv()
    each(1, 4, lambda r: c2_x(r).start())

    row = lax.broadcasted_iota(jnp.int32, (64, 64), 0)
    hour = lax.broadcasted_iota(jnp.int32, (64, 64), 1)
    evens_first = hour == jnp.where(row < 32, 2 * row, 2 * row - 63)
    c3_out[...] = jnp.dot(
        evens_first.astype(BF16), c3_ref[...], preferred_element_type=F32
    ).astype(BF16)
    ring(4)

    each(1, N, lambda r: a1_copy(r).wait_recv())
    each(1, N, lambda r: t2_copy(r).wait_recv())
    three = jnp.sum(a1r[:, 2], axis=0)
    for k in range(4):
        g2s[k] = three[k : k + 1]
    g2s[4] = jnp.sum(t2r[...], axis=0)
    each(1, N, lambda r: g2_copy(r).start())
    g2r[mx] = g2s[...]

    each(0, N, lambda r: f_x(r).wait_recv())
    f_x_core.start()
    one_out[0:4] = jnp.sum(a1r[:, 0], axis=0)
    one_out[4:8] = jnp.sum(a1r[:, 1], axis=0)
    each(1, 4, lambda r: c2_x(r).wait_recv())
    c2_core.start()

    def add_shard(g):
        acc[...] += jnp.dot(fall[g].reshape(256, 96), cfall[g], preferred_element_type=F32)

    acc[...] = jnp.zeros_like(acc)
    f_core.wait_recv()
    f_x_core.wait_recv()
    for o in OFFSETS:
        add_shard(shard(o, ylo))
        y_copy(o, 0).wait_recv()
        y_copy(o, 1).wait_recv()
        add_shard(shard(o, 1 - ylo))
    acct[...] = acc[...].T

    def m_copy(m):
        return send(fms.at[m], fmr.at[four], p2s.at[m], p2r.at[four], (4 * quarter + m, mx))

    def stays(m):
        return jnp.logical_and(4 * quarter + m == mx, mx == my)

    for m in range(4):
        fms[m] = acct[50 * m : 50 * m + BLK, :].astype(BF16)

        @pl.when(jnp.logical_not(stays(m)))
        def _():
            m_copy(m).start()

        @pl.when(stays(m))
        def _():
            fmr[four] = fms[m]

    each(1, N, lambda r: g2_copy(r).wait_recv())
    g3s[...] = jnp.concatenate([jnp.sum(g2r[:, k], axis=0) for k in range(4)], axis=0)
    each(1, N, lambda r: g3_copy(r).start())
    g3r[my] = g3s[...]
    for g in range(N):
        two_out[g : g + 1] = g2r[g, 4]
    c2_core.wait_recv()

    sent_quarter = mx // 4
    from_self = jnp.logical_and(mx == my, sent_quarter == quarter)

    def first_arrives(s):
        @pl.when(jnp.logical_not(jnp.logical_and(from_self, s == four)))
        def _():
            send(fms.at[0], fmr.at[s], p2s.at[0], p2r.at[s], other_core).wait_recv()

    each(0, 4, first_arrives)
    for s in range(4):
        part = fmr[s].astype(F32)
        for t in range(4):
            lhsf[BLK * t : BLK * t + BLK, BLK * s : BLK * s + BLK] = part[:, BLK * t : BLK * t + BLK]
    lhs = lhsf[...].astype(BF16)
    low_lanes = lax.broadcasted_iota(jnp.int32, (BLK, 128), 1) < BLK
    for u in range(4):
        rhs = c2all[:, :, :, :, 256 * u : 256 * u + 256].reshape(256, 256)
        got = jnp.dot(lhs, rhs, preferred_element_type=F32)
        for v in range(2):
            for p in range(2):
                first = got[2 * BLK * p : 2 * BLK * p + BLK, 128 * v : 128 * v + 128]
                second = got[2 * BLK * p + BLK : 2 * BLK * p + 2 * BLK, 128 * v : 128 * v + 128]
                g = 4 * u + 2 * v
                sms[g, p] = jnp.where(low_lanes, first, pltpu.roll(second, BLK, 1)).astype(BF16)
                sms[g + 1, p] = jnp.where(low_lanes, pltpu.roll(first, BLK, 1), second).astype(BF16)

    def p3_copy(r):
        return send(
            sms.at[gy_peer(r)], rr.at[pl.ds(2 * my, 2)], p3s.at[r], p3r.at[r], (mx, gy_peer(r))
        )

    each(1, N, lambda r: p3_copy(r).start())
    rr[pl.ds(2 * my, 2)] = sms[my]

    each(1, N, lambda r: g3_copy(r).wait_recv())
    for g in range(N):
        three_out[4 * g : 4 * g + 4] = g3r[g]

    for step in range(1, 5):
        z_copy(1, step).wait_send()
    for step in range(1, 4):
        z_copy(-1, step).wait_send()
    for o in OFFSETS:
        y_copy(o, 0).wait_send()
        y_copy(o, 1).wait_send()
    c2_y.wait_send()
    each(1, 4, lambda r: c2_x(r).wait_send())
    c2_core.wait_send()
    f_core.wait_send()
    f_x_core.wait_send()
    f_x(0).wait_send()

    def left(r):
        f_copy(r).wait_send()
        f_x(r).wait_send()
        a1_copy(r).wait_send()
        t2_copy(r).wait_send()
        g2_copy(r).wait_send()
        g3_copy(r).wait_send()

    each(1, N, left)
    for m in range(4):

        @pl.when(jnp.logical_not(stays(m)))
        def _():
            m_copy(m).wait_send()

    each(1, N, lambda r: p3_copy(r).wait_recv())
    rr_out[...] = rr[...]
    each(1, N, lambda r: p3_copy(r).wait_send())


CHUNK = 10


def hours_kernel(
    rr_ref, c3_ref, m1_ref, m2_ref, m3_ref, core_out, one_out, two_out, three_out, rrf, lhs
):
    step = pl.program_id(0)

    @pl.when(step == 0)
    def _():
        for r in range(32):
            rrf[BLK * r : BLK * r + BLK, :] = rr_ref[r].astype(F32)
        one_out[...] = m1_ref[0:6, :]
        two_out[...] = m2_ref[...]
        three_out[...] = m3_ref[...]

    for k in range(CHUNK):
        turned = rrf[pl.ds(step * CHUNK + k, 32, stride=BLK), :].T
        lhs[56 * k : 56 * k + 56, 0:32] = turned[0:56]
        lhs[56 * k : 56 * k + 56, 32:64] = turned[BLK : BLK + 56]
    got = jnp.dot(lhs[...].astype(BF16), c3_ref[...], preferred_element_type=F32)
    for k in range(CHUNK):
        core_out[k] = got[56 * k : 56 * k + 50]


def on_device(
    field_slab, one_by_second, one_by_hours, two_by_first, two_by_hours,
    three_by_first, three_by_second, core_first, core_second, core_hours,
):
    vmem = pl.BlockSpec(memory_space=pltpu.VMEM)
    hbm = pl.BlockSpec(memory_space=pltpu.HBM)
    dma = pltpu.SemaphoreType.DMA
    arguments = (
        jnp.transpose(field_slab, (1, 2, 0)), core_first.T, core_second.T, core_hours.T,
        one_by_second, one_by_hours, two_by_first, two_by_hours, three_by_first, three_by_second,
    )
    sizes = (
        ((32, BLK, 128), BF16), ((64, 800), BF16), ((8, 400), F32), ((16, 400), F32), ((64, 400), F32)
    )
    ways = [10, 16, 16, 16, 16, 2, 2, 7, 7, 16, 16, 5, 5, 4, 4, 16, 16] + [16] * 8
    between = pl.pallas_call(
        exchange_kernel,
        out_shape=tuple(jax.ShapeDtypeStruct(shape, dtype) for shape, dtype in sizes),
        in_specs=[hbm] * 10,
        out_specs=(vmem,) * 5,
        scratch_shapes=[pltpu.VMEM(a.shape, a.dtype) for a in arguments]
        + [
            pltpu.VMEM((1024, 128), F32),
            pltpu.VMEM((N, 4, 16, 96), BF16),
            pltpu.VMEM((N, 4, 4, 16, 96), BF16),
            pltpu.VMEM((N, 96, WIN), BF16),
            pltpu.VMEM((16, 1024), F32),
            pltpu.VMEM((4, 2, 2, 16, 1024), BF16),
            pltpu.VMEM((16, 400), F32),
            pltpu.VMEM((16, 400), F32),
            pltpu.VMEM((256, WIN), F32),
            pltpu.VMEM((WIN, 256), F32),
            pltpu.VMEM((4, BLK, 256), BF16),
            pltpu.VMEM((4, BLK, 256), BF16),
            pltpu.VMEM((256, 256), F32),
            pltpu.VMEM((N, 2, BLK, 128), BF16),
            pltpu.VMEM((32, BLK, 128), BF16),
            pltpu.VMEM((96, 400), F32),
            pltpu.VMEM((16, 400), F32),
            pltpu.VMEM((64, 400), F32),
            pltpu.VMEM((N, 3, 4, 400), F32),
            pltpu.VMEM((N, 3, 4, 400), F32),
            pltpu.VMEM((N, 1, 400), F32),
            pltpu.VMEM((N, 1, 400), F32),
            pltpu.VMEM((5, 1, 400), F32),
            pltpu.VMEM((N, 5, 1, 400), F32),
            pltpu.VMEM((4, 400), F32),
            pltpu.VMEM((N, 4, 400), F32),
        ]
        + [dma((n,)) for n in ways],
        compiler_params=pltpu.CompilerParams(
            collective_id=0, has_side_effects=True, vmem_limit_bytes=60 * 2**20
        ),
        cost_estimate=pl.CostEstimate(flops=500_000_000, bytes_accessed=2_000_000, transcendentals=0),
        name="exchange",
    )(*arguments)

    def whole(shape):
        return pl.BlockSpec(shape, lambda step: (0,) * len(shape))

    core_sketch, mode_one, mode_two, mode_three = pl.pallas_call(
        hours_kernel,
        grid=(50 // CHUNK,),
        out_shape=(
            jax.ShapeDtypeStruct((50, 50, 800), F32),
            jax.ShapeDtypeStruct((6, 400), F32),
            jax.ShapeDtypeStruct((16, 400), F32),
            jax.ShapeDtypeStruct((64, 400), F32),
        ),
        in_specs=[whole(shape) for shape, _ in sizes],
        out_specs=(
            pl.BlockSpec((CHUNK, 50, 800), lambda step: (step, 0, 0)),
            whole((6, 400)), whole((16, 400)), whole((64, 400)),
        ),
        scratch_shapes=[
            pltpu.VMEM((32 * BLK, 128), F32),
            pltpu.VMEM((56 * CHUNK, 64), F32),
        ],
        compiler_params=pltpu.CompilerParams(vmem_limit_bytes=60 * 2**20),
        cost_estimate=pl.CostEstimate(flops=260_000_000, bytes_accessed=11_000_000, transcendentals=0),
        name="hours",
    )(*between)
    return mode_one, mode_two, mode_three, core_sketch


def solution(mesh):
    in_specs = (
        P("gx", "gy", None),
        P("gy", None),
        P(),
        P("gx", None),
        P(),
        P("gx", None),
        P("gy", None),
        P(None, "gx"),
        P(None, "gy"),
        P(),
    )
    out_specs = (P(("gx", "gy"), None), P("gy", None), P(), P("gx", "gy", None))
    return jax.shard_map(
        on_device, mesh=mesh, in_specs=in_specs, out_specs=out_specs, check_vma=False
    )
```

time: 75.9 us -> 62.4 us (0.82)
  local copies, waits for them, and re-layouts: 8.4 us -> 0 us
  Pallas kernels: 66.1 us -> 61.6 us
    unnamed x20 -> x0, local copies, waits for them, and re-layouts: 8.4 us -> none
    pallas_call x1, Pallas kernels: 59.8 us -> 54.3 us  [on_device(): pl.pallas_call(exchange_kernel, out_shape=tuple((jax.ShapeDtypeStruct(sha...]
    pallas_call x1, Pallas kernels: 6.3 us -> 7.35 us  [on_device(): pl.pallas_call(hours_kernel, grid=(50 // CHUNK,), out_shape=(jax.ShapeDty...]
where the time goes in v2:
time: 62.4 us; the launch traced here: 62.3 us
  Pallas kernels  61.6 us (99%)
  between operations  0.64 us (1%)
    pallas_call x1, Pallas kernels, on_device(): pl.pallas_call(exchange_kernel, out_shape=tuple((jax.ShapeDtypeStruct(sha...  54.3 us
    pallas_call x1, Pallas kernels, on_device(): pl.pallas_call(hours_kernel, grid=(50 // CHUNK,), out_shape=(jax.ShapeDty...  7.35 us

profile of v2, /device:TPU:1, one launch (start us, length us, event | category | flops | bytes accessed | tf_op | source)
XLA Modules:
  0.0 62.3 jit_solution(9700609522230043064)
XLA Ops:
  0.6 54.3 %exchange.1 = (bf16[32,64,128]{2,1,0:T(8,128)(2,1)}, bf16[64,800]{1,0:T(8,128)(2,1)}, f32[8,400]{1,0:T(8,128)}, f32[16,400]{1,0:T(8,128)}, f32[64,400]{1,0:T(8,128)}) custom-call(bf16[16,64,96]{2,1,0:T(8,128)(2,1)} %bitcast.4, bf16[96,800]{1,0:T(8,128)(2,1)} %bitcast.5, bf16[16,800]{1,0:T(8,128)(2,1)} %bitcast.7, bf16[64,800]{1,0:T(8,128)(2,1)} %bitcast.6, ...), custom_call_target="tpu_custom_call" | custom-call | flops 500000000 | bytes 2000000 | tf_op jit(solution)/shard_map/exchange/pallas_call | solution.py:401
  54.9 7.3 %hours.1 = (f32[50,50,800]{2,1,0:T(8,128)}, f32[6,400]{1,0:T(8,128)}, f32[16,400]{1,0:T(8,128)}, f32[64,400]{1,0:T(8,128)}) custom-call(bf16[32,64,128]{2,1,0:T(8,128)(2,1)} %get-tuple-element.13.rr_ref, bf16[64,800]{1,0:T(8,128)(2,1)} %get-tuple-element.14.c3_ref, f32[8,400]{1,0:T(8,128)} %get-tuple-element.15.m1_ref, f32[16,400]{1,0:T(8,128)} %get-tuple-element.16.m2_ref, ...), custom_call_target="tpu_custom_call" | custom-call | flops 260000000 | bytes 11000000 | tf_op jit(solution)/shard_map/hours/pallas_call | solution.py:446

commit v3 on v2

--- a/solution.py
+++ b/solution.py
@@ -11,6 +11,7 @@
 N = 16
 NZ = 8
 WIN = 256
+ROWS = 112
 BLK = 64
 OFFSETS = (0, -1, 1, -2, 2, -3, 3, -4)
 
@@ -19,10 +20,10 @@
     f_hbm, cf_hbm, c2_hbm, c3_hbm, s1_hbm, h1_hbm, f2_hbm, h2_hbm, f3_hbm, s3_hbm,
     rr_out, c3_out, one_out, two_out, three_out,
     f_ref, cf_ref, c2_ref, c3_ref, s1_ref, h1_ref, f2_ref, h2_ref, f3_ref, s3_ref,
-    f32s, fblk, fall, cfall, c2f, c2all, s1f, s3f, acc, acct, fms, fmr, lhsf, sms, rr,
-    m1a, m2a, m3a, a1s, a1r, t2s, t2r, g2s, g2r, g3s, g3r,
-    loads, fs, fr, fxs, fxr, fcs, fcr, zs, zr, ys, yr, cs, cr, p2s, p2r, p3s, p3r,
-    a1ss, a1rs, t2ss, t2rs, g2ss, g2rs, g3ss, g3rs,
+    f32s, fblk, fall, cfall, c2f, c2all, s1f, s3f, acct, fms, fmr, lhsf, sms, rr,
+    c3v, onev, twov, threev, m1a, m2a, m3a, m1s, m1r, t3s, t3r, t2s, t2r, g2s, g2r, g3s, g3r,
+    loads, stores, keeps, fs, fr, fxs, fxr, fxcs, fxcr, fcs, fcr, zs, zr, ys, yr, cs, cr, p2s, p2r, p3s, p3r,
+    m1ss, m1rs, t3ss, t3rs, t2ss, t2rs, g2ss, g2rs, g3ss, g3rs,
 ):
     mx, my = lax.axis_index("gx"), lax.axis_index("gy")
     ylo, z = lax.rem(mx, 2), mx // 2
@@ -67,6 +68,8 @@
     load = [pltpu.make_async_copy(src, dst, loads.at[i]) for i, (src, dst) in enumerate(pairs)]
     for one in load:
         one.start()
+    results = ((c3v, c3_out), (onev, one_out), (twov, two_out), (threev, three_out))
+    store = [pltpu.make_async_copy(src, dst, stores.at[i]) for i, (src, dst) in enumerate(results)]
 
     barrier = pltpu.get_barrier_semaphore()
 
@@ -89,10 +92,15 @@
     load[0].wait()
     for j in range(16):
         f32s[64 * j : 64 * j + 64, 0:96] = f_ref[j].astype(F32)
-    for t in range(64):
-        fblk[t // 4, t % 4] = f32s[pl.ds(t, 16, stride=64), :][:, 0:96].astype(BF16)
-    for t in range(4):
-        fall[mx, t, quarter] = fblk[mx, t]
+    for g in range(N):
+        last = f32s[pl.ds(4 * g + 3, 16, stride=64), :]
+        for k in range(3):
+            rows = f32s[pl.ds(4 * g + k, 16, stride=64), :]
+            fblk[g, k] = jnp.concatenate(
+                [rows[:, 0:96], last[:, 32 * k : 32 * k + 32]], axis=1
+            ).astype(BF16)
+    for k in range(3):
+        fall[mx, k, quarter] = fblk[mx, k]
 
     pl.semaphore_wait(barrier, 2 * (N - 1) + 1)
 
@@ -136,8 +144,27 @@
 
     own_columns = fall.at[:, :, quarter]
     f_core = send(own_columns, own_columns, fcs.at[0], fcr.at[0], other_core)
-    x_columns = fall.at[:, :, quarter + 2 - 4 * xlo]
-    f_x_core = send(x_columns, x_columns, fcs.at[1], fcr.at[1], other_core)
+
+    def f_x_core(r):
+        slot = fall.at[lax.rem(mx + N - r, N), :, quarter + 2 - 4 * xlo]
+        return send(slot, slot, fxcs.at[r], fxcr.at[r], other_core)
+
+    def x_arrives(r):
+        f_x(r).wait_recv()
+        f_x_core(r).start()
+
+
+    c2_own = c2all.at[four, xlo, core]
+    c2_y = send(c2_own, c2_own, cs.at[0], cr.at[0], (mx, my + 2 - 4 * yhi))
+
+    def c2_x(r):
+        pair = c2all.at[pl.ds(2 * xhi, 2), xlo, core]
+        return send(
+            pair, pair, cs.at[r], cr.at[r], (mx, 4 * lax.rem(x + r, 4) + 2 * yhi + core)
+        )
+
+    c2_mine = c2all.at[:, :, core]
+    c2_core = send(c2_mine, c2_mine, cs.at[4], cr.at[4], other_core)
 
     z_copy(1, 1).start()
     z_copy(-1, 1).start()
@@ -169,8 +196,11 @@
     ring(1)
     modes(8, 16)
 
-    def a1_copy(r):
-        return send(a1s.at[gy_peer(r)], a1r.at[my], a1ss.at[r], a1rs.at[r], (mx, gy_peer(r)))
+    def m1_copy(r):
+        return send(m1s.at[gy_peer(r)], m1r.at[my], m1ss.at[r], m1rs.at[r], (mx, gy_peer(r)))
+
+    def t3_copy(r):
+        return send(t3s.at[gy_peer(r)], t3r.at[my], t3ss.at[r], t3rs.at[r], (mx, gy_peer(r)))
 
     def t2_copy(r):
         return send(t2s.at[gx_peer(r)], t2r.at[mx], t2ss.at[r], t2rs.at[r], (gx_peer(r), my))
@@ -181,19 +211,19 @@
     def g3_copy(r):
         return send(g3s, g3r.at[my], g3ss.at[r], g3rs.at[r], (mx, gy_peer(r)))
 
-    a1s[:, 1] = jnp.zeros((N, 4, 400), F32)
+    m1s[:, 1] = jnp.zeros((N, 4, 400), F32)
     for g in range(N):
-        a1s[g, 0] = m1a[6 * g : 6 * g + 4]
-        a1s[g, 1, 0:2] = m1a[6 * g + 4 : 6 * g + 6]
-        a1s[g, 2] = m3a[4 * g : 4 * g + 4]
+        m1s[g, 0] = m1a[6 * g : 6 * g + 4]
+        m1s[g, 1, 0:2] = m1a[6 * g + 4 : 6 * g + 6]
+        t3s[g] = m3a[4 * g : 4 * g + 4]
         t2s[g] = m2a[g : g + 1]
 
     def first_exchange(r):
         t2_copy(r).start()
-        a1_copy(r).start()
+        t3_copy(r).start()
 
     each(1, N, first_exchange)
-    a1r[my] = a1s[my]
+    t3r[my] = t3s[my]
     t2r[mx] = t2s[mx]
     ring(2)
 
@@ -201,18 +231,7 @@
     for g in range(N):
         c2f[:, BLK * g : BLK * g + 50] = c2_ref[:, 50 * g : 50 * g + 50].astype(F32)
     c2all[four, xlo, core] = c2f[...].astype(BF16)
-    c2_own = c2all.at[four, xlo, core]
-    c2_y = send(c2_own, c2_own, cs.at[0], cr.at[0], (mx, my + 2 - 4 * yhi))
     c2_y.start()
-
-    def c2_x(r):
-        pair = c2all.at[pl.ds(2 * xhi, 2), xlo, core]
-        return send(
-            pair, pair, cs.at[r], cr.at[r], (mx, 4 * lax.rem(x + r, 4) + 2 * yhi + core)
-        )
-
-    c2_mine = c2all.at[:, :, core]
-    c2_core = send(c2_mine, c2_mine, cs.at[4], cr.at[4], other_core)
 
     def field_arrives(r):
         f_copy(r).wait_recv()
@@ -226,40 +245,44 @@
 
     row = lax.broadcasted_iota(jnp.int32, (64, 64), 0)
     hour = lax.broadcasted_iota(jnp.int32, (64, 64), 1)
-    evens_first = hour == jnp.where(row < 32, 2 * row, 2 * row - 63)
-    c3_out[...] = jnp.dot(
-        evens_first.astype(BF16), c3_ref[...], preferred_element_type=F32
+    arranged = hour == 4 * (row & 15) + 2 * ((row >> 4) & 1) + (row >> 5)
+    c3v[...] = jnp.dot(
+        arranged.astype(BF16), c3_ref[...], preferred_element_type=F32
     ).astype(BF16)
+    store[0].start()
     ring(4)
 
-    each(1, N, lambda r: a1_copy(r).wait_recv())
+    each(1, N, lambda r: t3_copy(r).wait_recv())
     each(1, N, lambda r: t2_copy(r).wait_recv())
-    three = jnp.sum(a1r[:, 2], axis=0)
+    three = jnp.sum(t3r[...], axis=0)
     for k in range(4):
         g2s[k] = three[k : k + 1]
     g2s[4] = jnp.sum(t2r[...], axis=0)
     each(1, N, lambda r: g2_copy(r).start())
     g2r[mx] = g2s[...]
 
-    each(0, N, lambda r: f_x(r).wait_recv())
-    f_x_core.start()
-    one_out[0:4] = jnp.sum(a1r[:, 0], axis=0)
-    one_out[4:8] = jnp.sum(a1r[:, 1], axis=0)
+    each(0, N, x_arrives)
     each(1, 4, lambda r: c2_x(r).wait_recv())
     c2_core.start()
 
-    def add_shard(g):
-        acc[...] += jnp.dot(fall[g].reshape(256, 96), cfall[g], preferred_element_type=F32)
-
-    acc[...] = jnp.zeros_like(acc)
+    def total(side, wait):
+        got = jnp.zeros((128, WIN), F32)
+        for o in OFFSETS:
+            for low in range(2):
+                g = shard(o, (ylo + low) % 2)
+                if low and wait:
+                    y_copy(o, 0).wait_recv()
+                    y_copy(o, 1).wait_recv()
+                three = fall[g, :, pl.ds(2 * side, 2)].reshape(3, 32, 128)
+                last = jnp.concatenate([three[k, :, 96:128] for k in range(3)], axis=1)
+                rows = jnp.concatenate([three[k, :, 0:96] for k in range(3)] + [last], axis=0)
+                got += jnp.dot(rows, cfall[g], preferred_element_type=F32)
+        acct[side] = got.T
+
     f_core.wait_recv()
-    f_x_core.wait_recv()
-    for o in OFFSETS:
-        add_shard(shard(o, ylo))
-        y_copy(o, 0).wait_recv()
-        y_copy(o, 1).wait_recv()
-        add_shard(shard(o, 1 - ylo))
-    acct[...] = acc[...].T
+    total(xlo, True)
+    each(0, N, lambda r: f_x_core(r).wait_recv())
+    total(1 - xlo, False)
 
     def m_copy(m):
         return send(fms.at[m], fmr.at[four], p2s.at[m], p2r.at[four], (4 * quarter + m, mx))
@@ -268,7 +291,8 @@
         return jnp.logical_and(4 * quarter + m == mx, mx == my)
 
     for m in range(4):
-        fms[m] = acct[50 * m : 50 * m + BLK, :].astype(BF16)
+        rows = slice(50 * m, 50 * m + BLK)
+        fms[m] = jnp.concatenate([acct[0, rows], acct[1, rows]], axis=1).astype(BF16)
 
         @pl.when(jnp.logical_not(stays(m)))
         def _():
@@ -277,13 +301,17 @@
         @pl.when(stays(m))
         def _():
             fmr[four] = fms[m]
+
+    each(1, N, lambda r: m1_copy(r).start())
+    m1r[my] = m1s[my]
 
     each(1, N, lambda r: g2_copy(r).wait_recv())
     g3s[...] = jnp.concatenate([jnp.sum(g2r[:, k], axis=0) for k in range(4)], axis=0)
     each(1, N, lambda r: g3_copy(r).start())
     g3r[my] = g3s[...]
     for g in range(N):
-        two_out[g : g + 1] = g2r[g, 4]
+        twov[g : g + 1] = g2r[g, 4]
+    store[2].start()
     c2_core.wait_recv()
 
     sent_quarter = mx // 4
@@ -298,31 +326,50 @@
     for s in range(4):
         part = fmr[s].astype(F32)
         for t in range(4):
-            lhsf[BLK * t : BLK * t + BLK, BLK * s : BLK * s + BLK] = part[:, BLK * t : BLK * t + BLK]
+            for side in range(2):
+                to, at = BLK * s + 32 * side, 128 * side + 32 * t
+                lhsf[BLK * t : BLK * t + BLK, to : to + 32] = part[:, at : at + 32]
     lhs = lhsf[...].astype(BF16)
     low_lanes = lax.broadcasted_iota(jnp.int32, (BLK, 128), 1) < BLK
-    for u in range(4):
-        rhs = c2all[:, :, :, :, 256 * u : 256 * u + 256].reshape(256, 256)
+    def p3_copy(g):
+        return send(sms.at[g], rr.at[my], p3s.at[g], p3r.at[my], (mx, g))
+
+    for ahead in (2, 1, 3, 0):
+        u = lax.rem(x + ahead, 4)
+        columns = pl.ds(pl.multiple_of(256 * u, 256), 256)
+        rhs = c2all[:, :, :, :, columns].reshape(256, 256)
         got = jnp.dot(lhs, rhs, preferred_element_type=F32)
         for v in range(2):
+            g = 4 * u + 2 * v
+            lower, upper = [], []
             for p in range(2):
-                first = got[2 * BLK * p : 2 * BLK * p + BLK, 128 * v : 128 * v + 128]
-                second = got[2 * BLK * p + BLK : 2 * BLK * p + 2 * BLK, 128 * v : 128 * v + 128]
-                g = 4 * u + 2 * v
-                sms[g, p] = jnp.where(low_lanes, first, pltpu.roll(second, BLK, 1)).astype(BF16)
-                sms[g + 1, p] = jnp.where(low_lanes, pltpu.roll(first, BLK, 1), second).astype(BF16)
-
-    def p3_copy(r):
-        return send(
-            sms.at[gy_peer(r)], rr.at[pl.ds(2 * my, 2)], p3s.at[r], p3r.at[r], (mx, gy_peer(r))
-        )
-
-    each(1, N, lambda r: p3_copy(r).start())
-    rr[pl.ds(2 * my, 2)] = sms[my]
-
+                tile = slice(128 * v, 128 * v + 128)
+                first = got[2 * BLK * p : 2 * BLK * p + BLK, tile]
+                second = got[2 * BLK * p + BLK : 2 * BLK * p + 2 * BLK, tile]
+                lower.append(jnp.where(low_lanes, first, pltpu.roll(second, BLK, 1))[0:50])
+                upper.append(jnp.where(low_lanes, pltpu.roll(first, BLK, 1), second)[0:50])
+            fill = [jnp.zeros((ROWS - 100, 128), F32)]
+            sms[g] = jnp.concatenate(lower + fill, axis=0).astype(BF16)
+            sms[g + 1] = jnp.concatenate(upper + fill, axis=0).astype(BF16)
+            for to in (g, g + 1):
+                if ahead:
+                    p3_copy(to).start()
+                else:
+
+                    @pl.when(to != my)
+                    def _():
+                        p3_copy(to).start()
+
+    rr[my] = sms[my]
+
+    each(1, N, lambda r: m1_copy(r).wait_recv())
+    onev[0:4] = jnp.sum(m1r[:, 0], axis=0)
+    onev[4:6] = jnp.sum(m1r[:, 1], axis=0)[0:2]
+    store[1].start()
     each(1, N, lambda r: g3_copy(r).wait_recv())
     for g in range(N):
-        three_out[4 * g : 4 * g + 4] = g3r[g]
+        threev[4 * g : 4 * g + 4] = g3r[g]
+    store[3].start()
 
     for step in range(1, 5):
         z_copy(1, step).wait_send()
@@ -335,13 +382,15 @@
     each(1, 4, lambda r: c2_x(r).wait_send())
     c2_core.wait_send()
     f_core.wait_send()
-    f_x_core.wait_send()
     f_x(0).wait_send()
+    f_x_core(0).wait_send()
 
     def left(r):
         f_copy(r).wait_send()
         f_x(r).wait_send()
-        a1_copy(r).wait_send()
+        f_x_core(r).wait_send()
+        m1_copy(r).wait_send()
+        t3_copy(r).wait_send()
         t2_copy(r).wait_send()
         g2_copy(r).wait_send()
         g3_copy(r).wait_send()
@@ -353,41 +402,70 @@
         def _():
             m_copy(m).wait_send()
 
-    each(1, N, lambda r: p3_copy(r).wait_recv())
-    rr_out[...] = rr[...]
-    each(1, N, lambda r: p3_copy(r).wait_send())
-
-
-CHUNK = 10
+    def second_arrives(r):
+        send(sms.at[0], rr.at[0], p3s.at[0], p3r.at[gy_peer(r)], other_core).wait_recv()
+        keep(gy_peer(r)).start()
+
+    def keep(g):
+        return pltpu.make_async_copy(rr.at[g], rr_out.at[g], keeps.at[g])
+
+    keep(my).start()
+    each(1, N, second_arrives)
+    for one in store:
+        one.wait()
+    each(0, N, lambda g: keep(g).wait())
+    each(1, N, lambda r: p3_copy(gy_peer(r)).wait_send())
+
+
+CHUNKS = (3, 5, 8, 10, 12, 12)
 
 
 def hours_kernel(
-    rr_ref, c3_ref, m1_ref, m2_ref, m3_ref, core_out, one_out, two_out, three_out, rrf, lhs
+    rr_hbm, c3_hbm, m1_hbm, m2_hbm, m3_hbm, core_out, one_out, two_out, three_out,
+    rr_ref, c3_ref, m1_ref, m2_ref, m3_ref, rrf, lhs, core_ref, loads, passes, stores,
 ):
-    step = pl.program_id(0)
-
-    @pl.when(step == 0)
-    def _():
-        for r in range(32):
-            rrf[BLK * r : BLK * r + BLK, :] = rr_ref[r].astype(F32)
-        one_out[...] = m1_ref[0:6, :]
-        two_out[...] = m2_ref[...]
-        three_out[...] = m3_ref[...]
-
-    for k in range(CHUNK):
-        turned = rrf[pl.ds(step * CHUNK + k, 32, stride=BLK), :].T
-        lhs[56 * k : 56 * k + 56, 0:32] = turned[0:56]
-        lhs[56 * k : 56 * k + 56, 32:64] = turned[BLK : BLK + 56]
-    got = jnp.dot(lhs[...].astype(BF16), c3_ref[...], preferred_element_type=F32)
-    for k in range(CHUNK):
-        core_out[k] = got[56 * k : 56 * k + 50]
+    get_rr = pltpu.make_async_copy(rr_hbm, rr_ref, loads.at[0])
+    get_c3 = pltpu.make_async_copy(c3_hbm, c3_ref, loads.at[1])
+    get_rr.start()
+    get_c3.start()
+    modes = ((m1_hbm, m1_ref, one_out), (m2_hbm, m2_ref, two_out), (m3_hbm, m3_ref, three_out))
+    taken = [pltpu.make_async_copy(a, b, passes.at[i]) for i, (a, b, _) in enumerate(modes)]
+    passed = [pltpu.make_async_copy(b, c, passes.at[3 + i]) for i, (_, b, c) in enumerate(modes)]
+    for one in taken:
+        one.start()
+    get_rr.wait()
+    for g in range(N):
+        rrf[ROWS * g : ROWS * g + ROWS, :] = rr_ref[g].astype(F32)
+    get_c3.wait()
+    for i in range(3):
+        taken[i].wait()
+        passed[i].start()
+
+    stored, done = [], 0
+    for i, chunk in enumerate(CHUNKS):
+        for a in range(done, done + chunk):
+            hours = [rrf[pl.ds(50 * p + a, N, stride=ROWS), :] for p in range(2)]
+            turned = jnp.concatenate(hours, axis=0).T
+            lhs[56 * a : 56 * a + 56, 0:32] = turned[0:56]
+            lhs[56 * a : 56 * a + 56, 32:64] = turned[BLK : BLK + 56]
+        got = jnp.dot(
+            lhs[56 * done : 56 * (done + chunk)].astype(BF16), c3_ref[...],
+            preferred_element_type=F32,
+        )
+        for k in range(chunk):
+            core_ref[done + k] = got[56 * k : 56 * k + 50]
+        rows = pl.ds(done, chunk)
+        stored.append(pltpu.make_async_copy(core_ref.at[rows], core_out.at[rows], stores.at[i]))
+        stored[-1].start()
+        done += chunk
+    for one in passed + stored:
+        one.wait()
 
 
 def on_device(
     field_slab, one_by_second, one_by_hours, two_by_first, two_by_hours,
     three_by_first, three_by_second, core_first, core_second, core_hours,
 ):
-    vmem = pl.BlockSpec(memory_space=pltpu.VMEM)
     hbm = pl.BlockSpec(memory_space=pltpu.HBM)
     dma = pltpu.SemaphoreType.DMA
     arguments = (
@@ -395,36 +473,41 @@
         one_by_second, one_by_hours, two_by_first, two_by_hours, three_by_first, three_by_second,
     )
     sizes = (
-        ((32, BLK, 128), BF16), ((64, 800), BF16), ((8, 400), F32), ((16, 400), F32), ((64, 400), F32)
+        ((N, ROWS, 128), BF16), ((64, 800), BF16), ((6, 400), F32), ((16, 400), F32), ((64, 400), F32)
     )
-    ways = [10, 16, 16, 16, 16, 2, 2, 7, 7, 16, 16, 5, 5, 4, 4, 16, 16] + [16] * 8
+    ways = [10, 4, 16, 16, 16, 16, 16, 16, 16, 1, 1, 7, 7, 16, 16, 5, 5, 4, 4, 16, 16] + [16] * 10
     between = pl.pallas_call(
         exchange_kernel,
         out_shape=tuple(jax.ShapeDtypeStruct(shape, dtype) for shape, dtype in sizes),
         in_specs=[hbm] * 10,
-        out_specs=(vmem,) * 5,
+        out_specs=(hbm,) * 5,
         scratch_shapes=[pltpu.VMEM(a.shape, a.dtype) for a in arguments]
         + [
             pltpu.VMEM((1024, 128), F32),
-            pltpu.VMEM((N, 4, 16, 96), BF16),
-            pltpu.VMEM((N, 4, 4, 16, 96), BF16),
+            pltpu.VMEM((N, 3, 16, 128), BF16),
+            pltpu.VMEM((N, 3, 4, 16, 128), BF16),
             pltpu.VMEM((N, 96, WIN), BF16),
             pltpu.VMEM((16, 1024), F32),
             pltpu.VMEM((4, 2, 2, 16, 1024), BF16),
             pltpu.VMEM((16, 400), F32),
             pltpu.VMEM((16, 400), F32),
-            pltpu.VMEM((256, WIN), F32),
-            pltpu.VMEM((WIN, 256), F32),
+            pltpu.VMEM((2, WIN, 128), F32),
             pltpu.VMEM((4, BLK, 256), BF16),
             pltpu.VMEM((4, BLK, 256), BF16),
             pltpu.VMEM((256, 256), F32),
-            pltpu.VMEM((N, 2, BLK, 128), BF16),
-            pltpu.VMEM((32, BLK, 128), BF16),
+            pltpu.VMEM((N, ROWS, 128), BF16),
+            pltpu.VMEM((N, ROWS, 128), BF16),
+            pltpu.VMEM((64, 800), BF16),
+            pltpu.VMEM((6, 400), F32),
+            pltpu.VMEM((16, 400), F32),
+            pltpu.VMEM((64, 400), F32),
             pltpu.VMEM((96, 400), F32),
             pltpu.VMEM((16, 400), F32),
             pltpu.VMEM((64, 400), F32),
-            pltpu.VMEM((N, 3, 4, 400), F32),
-            pltpu.VMEM((N, 3, 4, 400), F32),
+            pltpu.VMEM((N, 2, 4, 400), F32),
+            pltpu.VMEM((N, 2, 4, 400), F32),
+            pltpu.VMEM((N, 4, 400), F32),
+            pltpu.VMEM((N, 4, 400), F32),
             pltpu.VMEM((N, 1, 400), F32),
             pltpu.VMEM((N, 1, 400), F32),
             pltpu.VMEM((5, 1, 400), F32),
@@ -440,26 +523,26 @@
         name="exchange",
     )(*arguments)
 
-    def whole(shape):
-        return pl.BlockSpec(shape, lambda step: (0,) * len(shape))
-
     core_sketch, mode_one, mode_two, mode_three = pl.pallas_call(
         hours_kernel,
-        grid=(50 // CHUNK,),
         out_shape=(
             jax.ShapeDtypeStruct((50, 50, 800), F32),
             jax.ShapeDtypeStruct((6, 400), F32),
             jax.ShapeDtypeStruct((16, 400), F32),
             jax.ShapeDtypeStruct((64, 400), F32),
         ),
-        in_specs=[whole(shape) for shape, _ in sizes],
-        out_specs=(
-            pl.BlockSpec((CHUNK, 50, 800), lambda step: (step, 0, 0)),
-            whole((6, 400)), whole((16, 400)), whole((64, 400)),
-        ),
+        in_specs=[hbm] * 5,
+        out_specs=(hbm,) * 4,
         scratch_shapes=[
-            pltpu.VMEM((32 * BLK, 128), F32),
-            pltpu.VMEM((56 * CHUNK, 64), F32),
+            pltpu.VMEM((N, ROWS, 128), BF16),
+            pltpu.VMEM((64, 800), BF16),
+            pltpu.VMEM((6, 400), F32),
+            pltpu.VMEM((16, 400), F32),
+            pltpu.VMEM((64, 400), F32),
+            pltpu.VMEM((N * ROWS, 128), F32),
+            pltpu.VMEM((56 * 50, 64), F32),
+            pltpu.VMEM((50, 50, 800), F32),
+            dma((2,)), dma((6,)), dma((len(CHUNKS),)),
         ],
         compiler_params=pltpu.CompilerParams(vmem_limit_bytes=60 * 2**20),
         cost_estimate=pl.CostEstimate(flops=260_000_000, bytes_accessed=11_000_000, transcendentals=0),

time: 62.4 us -> 57.6 us (0.923)
  Pallas kernels: 61.6 us -> 56.8 us
    pallas_call x1, Pallas kernels: 54.3 us -> 51.2 us  [on_device(): pl.pallas_call(exchange_kernel, out_shape=tuple((jax.ShapeDtypeStruct(sha...]
    pallas_call x1, Pallas kernels: 7.35 us -> 5.59 us  [on_device(): pl.pallas_call(hours_kernel, out_shape=(jax.ShapeDtypeStruct((50, 50, 800...]
where the time goes in v3:
time: 57.6 us; the launch traced here: 57.5 us
  Pallas kernels  56.8 us (99%)
  between operations  0.64 us (1%)
    pallas_call x1, Pallas kernels, on_device(): pl.pallas_call(exchange_kernel, out_shape=tuple((jax.ShapeDtypeStruct(sha...  51.2 us
    pallas_call x1, Pallas kernels, on_device(): pl.pallas_call(hours_kernel, out_shape=(jax.ShapeDtypeStruct((50, 50, 800...  5.59 us

profile of v3, /device:TPU:1, one launch (start us, length us, event | category | flops | bytes accessed | tf_op | source)
XLA Modules:
  0.0 57.5 jit_solution(7542797110580730287)
XLA Ops:
  0.6 51.2 %exchange.1 = (bf16[16,112,128]{2,1,0:T(8,128)(2,1)}, bf16[64,800]{1,0:T(8,128)(2,1)}, f32[6,400]{1,0:T(8,128)}, f32[16,400]{1,0:T(8,128)}, f32[64,400]{1,0:T(8,128)}) custom-call(bf16[16,64,96]{2,1,0:T(8,128)(2,1)} %bitcast.4, bf16[96,800]{1,0:T(8,128)(2,1)} %bitcast.5, bf16[16,800]{1,0:T(8,128)(2,1)} %bitcast.7, bf16[64,800]{1,0:T(8,128)(2,1)} %bitcast.6, ...), custom_call_target="tpu_custom_call" | custom-call | flops 500000000 | bytes 2000000 | tf_op jit(solution)/shard_map/exchange/pallas_call | solution.py:479
  51.9 5.6 %hours.1 = (f32[50,50,800]{2,1,0:T(8,128)}, f32[6,400]{1,0:T(8,128)}, f32[16,400]{1,0:T(8,128)}, f32[64,400]{1,0:T(8,128)}) custom-call(bf16[16,112,128]{2,1,0:T(8,128)(2,1)} %get-tuple-element.13.rr_hbm, bf16[64,800]{1,0:T(8,128)(2,1)} %get-tuple-element.14.c3_hbm, f32[6,400]{1,0:T(8,128)} %get-tuple-element.15.m1_hbm, f32[16,400]{1,0:T(8,128)} %get-tuple-element.16.m2_hbm, ...), custom_call_target="tpu_custom_call" | custom-call | flops 260000000 | bytes 11000000 | tf_op jit(solution)/shard_map/hours/pallas_call | solution.py:526

commit v4 on v3

--- a/solution.py
+++ b/solution.py
@@ -55,11 +55,8 @@
         return lax.rem(my + r, N)
 
     def each(low, high, body):
-        def step(i, carry):
+        for i in range(low, high):
             body(i)
-            return carry
-
-        lax.fori_loop(low, high, step, 0)
 
     pairs = (
         (f_hbm, f_ref), (cf_hbm, cf_ref), (c2_hbm, c2_ref), (h1_hbm, h1_ref), (h2_hbm, h2_ref),
@@ -77,7 +74,8 @@
         pl.semaphore_signal(barrier, inc=1, device_id=(gx_peer(r), my), device_id_type=MESH)
         pl.semaphore_signal(barrier, inc=1, device_id=(mx, gy_peer(r)), device_id_type=MESH)
 
-    each(1, N, greet)
+    for r in (8, 9, 7, 10, 6, 11, 5, 12, 4, 13, 3, 14, 2, 15, 1):
+        greet(r)
     across = (mx + 1 - 2 * ylo, my + 2 - 4 * yhi)
     pl.semaphore_signal(barrier, inc=1, device_id=across, device_id_type=MESH)
 
@@ -99,8 +97,7 @@
             fblk[g, k] = jnp.concatenate(
                 [rows[:, 0:96], last[:, 32 * k : 32 * k + 32]], axis=1
             ).astype(BF16)
-    for k in range(3):
-        fall[mx, k, quarter] = fblk[mx, k]
+    fall[mx, quarter] = fblk[mx]
 
     pl.semaphore_wait(barrier, 2 * (N - 1) + 1)
 
@@ -135,18 +132,18 @@
 
     def f_copy(r):
         return send(
-            fblk.at[gx_peer(r)], fall.at[mx, :, quarter], fs.at[r], fr.at[r], (gx_peer(r), my)
+            fblk.at[gx_peer(r)], fall.at[mx, quarter], fs.at[r], fr.at[r], (gx_peer(r), my)
         )
 
     def f_x(r):
-        slot = fall.at[lax.rem(mx + N - r, N), :, quarter]
+        slot = fall.at[lax.rem(mx + N - r, N), quarter]
         return send(slot, slot, fxs.at[r], fxr.at[r], other_x)
 
-    own_columns = fall.at[:, :, quarter]
+    own_columns = fall.at[:, quarter]
     f_core = send(own_columns, own_columns, fcs.at[0], fcr.at[0], other_core)
 
     def f_x_core(r):
-        slot = fall.at[lax.rem(mx + N - r, N), :, quarter + 2 - 4 * xlo]
+        slot = fall.at[lax.rem(mx + N - r, N), quarter + 2 - 4 * xlo]
         return send(slot, slot, fxcs.at[r], fxcr.at[r], other_core)
 
     def x_arrives(r):
@@ -227,17 +224,16 @@
     t2r[mx] = t2s[mx]
     ring(2)
 
+    def field_arrives(r):
+        f_copy(r).wait_recv()
+        f_x(r).start()
+
+    each(1, N, field_arrives)
     c2f[...] = jnp.zeros_like(c2f)
     for g in range(N):
         c2f[:, BLK * g : BLK * g + 50] = c2_ref[:, 50 * g : 50 * g + 50].astype(F32)
     c2all[four, xlo, core] = c2f[...].astype(BF16)
     c2_y.start()
-
-    def field_arrives(r):
-        f_copy(r).wait_recv()
-        f_x(r).start()
-
-    each(1, N, field_arrives)
     f_core.start()
     ring(3)
     c2_y.wait_recv()
@@ -273,9 +269,10 @@
                 if low and wait:
                     y_copy(o, 0).wait_recv()
                     y_copy(o, 1).wait_recv()
-                three = fall[g, :, pl.ds(2 * side, 2)].reshape(3, 32, 128)
-                last = jnp.concatenate([three[k, :, 96:128] for k in range(3)], axis=1)
-                rows = jnp.concatenate([three[k, :, 0:96] for k in range(3)] + [last], axis=0)
+                pair = fall[g, pl.ds(2 * side, 2)]
+                three = [pair[:, k].reshape(32, 128) for k in range(3)]
+                last = jnp.concatenate([three[k][:, 96:128] for k in range(3)], axis=1)
+                rows = jnp.concatenate([three[k][:, 0:96] for k in range(3)] + [last], axis=0)
                 got += jnp.dot(rows, cfall[g], preferred_element_type=F32)
         acct[side] = got.T
 
@@ -485,7 +482,7 @@
         + [
             pltpu.VMEM((1024, 128), F32),
             pltpu.VMEM((N, 3, 16, 128), BF16),
-            pltpu.VMEM((N, 3, 4, 16, 128), BF16),
+            pltpu.VMEM((N, 4, 3, 16, 128), BF16),
             pltpu.VMEM((N, 96, WIN), BF16),
             pltpu.VMEM((16, 1024), F32),
             pltpu.VMEM((4, 2, 2, 16, 1024), BF16),

time: 57.6 us -> 56.9 us (0.988)
  Pallas kernels: 56.8 us -> 55.9 us
    pallas_call x1, Pallas kernels: 51.2 us -> 50.3 us  [on_device(): pl.pallas_call(exchange_kernel, out_shape=tuple((jax.ShapeDtypeStruct(sha...]
where the time goes in v4:
time: 56.9 us; the launch traced here: 56.5 us
  Pallas kernels  55.9 us (98%)
  between operations  0.64 us (1%)
    pallas_call x1, Pallas kernels, on_device(): pl.pallas_call(exchange_kernel, out_shape=tuple((jax.ShapeDtypeStruct(sha...  50.3 us
    pallas_call x1, Pallas kernels, on_device(): pl.pallas_call(hours_kernel, out_shape=(jax.ShapeDtypeStruct((50, 50, 800...  5.59 us

profile of v4, /device:TPU:1, one launch (start us, length us, event | category | flops | bytes accessed | tf_op | source)
XLA Modules:
  0.0 56.5 jit_solution(2605089214845872983)
XLA Ops:
  0.6 50.3 %exchange.1 = (bf16[16,112,128]{2,1,0:T(8,128)(2,1)}, bf16[64,800]{1,0:T(8,128)(2,1)}, f32[6,400]{1,0:T(8,128)}, f32[16,400]{1,0:T(8,128)}, f32[64,400]{1,0:T(8,128)}) custom-call(bf16[16,64,96]{2,1,0:T(8,128)(2,1)} %bitcast.4, bf16[96,800]{1,0:T(8,128)(2,1)} %bitcast.5, bf16[16,800]{1,0:T(8,128)(2,1)} %bitcast.7, bf16[64,800]{1,0:T(8,128)(2,1)} %bitcast.6, ...), custom_call_target="tpu_custom_call" | custom-call | flops 500000000 | bytes 2000000 | tf_op jit(solution)/shard_map/exchange/pallas_call | solution.py:476
  50.9 5.6 %hours.1 = (f32[50,50,800]{2,1,0:T(8,128)}, f32[6,400]{1,0:T(8,128)}, f32[16,400]{1,0:T(8,128)}, f32[64,400]{1,0:T(8,128)}) custom-call(bf16[16,112,128]{2,1,0:T(8,128)(2,1)} %get-tuple-element.13.rr_hbm, bf16[64,800]{1,0:T(8,128)(2,1)} %get-tuple-element.14.c3_hbm, f32[6,400]{1,0:T(8,128)} %get-tuple-element.15.m1_hbm, f32[16,400]{1,0:T(8,128)} %get-tuple-element.16.m2_hbm, ...), custom_call_target="tpu_custom_call" | custom-call | flops 260000000 | bytes 11000000 | tf_op jit(solution)/shard_map/hours/pallas_call | solution.py:523

commit v5 on v4

--- a/solution.py
+++ b/solution.py
@@ -228,7 +228,8 @@
         f_copy(r).wait_recv()
         f_x(r).start()
 
-    each(1, N, field_arrives)
+    for r in (1, 15, 2, 14, 3, 13, 4, 12, 5, 11, 6, 10, 7, 9, 8):
+        field_arrives(r)
     c2f[...] = jnp.zeros_like(c2f)
     for g in range(N):
         c2f[:, BLK * g : BLK * g + 50] = c2_ref[:, 50 * g : 50 * g + 50].astype(F32)

time: 56.9 us -> 56.9 us (level)
  no operation moved by 1% of the time
where the time goes in v5:
time: 56.9 us; the launch traced here: 56.5 us
  Pallas kernels  55.9 us (98%)
  between operations  0.64 us (1%)
    pallas_call x1, Pallas kernels, on_device(): pl.pallas_call(exchange_kernel, out_shape=tuple((jax.ShapeDtypeStruct(sha...  50.3 us
    pallas_call x1, Pallas kernels, on_device(): pl.pallas_call(hours_kernel, out_shape=(jax.ShapeDtypeStruct((50, 50, 800...  5.59 us

profile of v5, /device:TPU:1, one launch (start us, length us, event | category | flops | bytes accessed | tf_op | source)
XLA Modules:
  0.0 56.5 jit_solution(8193080367711097914)
XLA Ops:
  0.6 50.3 %exchange.1 = (bf16[16,112,128]{2,1,0:T(8,128)(2,1)}, bf16[64,800]{1,0:T(8,128)(2,1)}, f32[6,400]{1,0:T(8,128)}, f32[16,400]{1,0:T(8,128)}, f32[64,400]{1,0:T(8,128)}) custom-call(bf16[16,64,96]{2,1,0:T(8,128)(2,1)} %bitcast.4, bf16[96,800]{1,0:T(8,128)(2,1)} %bitcast.5, bf16[16,800]{1,0:T(8,128)(2,1)} %bitcast.7, bf16[64,800]{1,0:T(8,128)(2,1)} %bitcast.6, ...), custom_call_target="tpu_custom_call" | custom-call | flops 500000000 | bytes 2000000 | tf_op jit(solution)/shard_map/exchange/pallas_call | solution.py:477
  50.9 5.6 %hours.1 = (f32[50,50,800]{2,1,0:T(8,128)}, f32[6,400]{1,0:T(8,128)}, f32[16,400]{1,0:T(8,128)}, f32[64,400]{1,0:T(8,128)}) custom-call(bf16[16,112,128]{2,1,0:T(8,128)(2,1)} %get-tuple-element.13.rr_hbm, bf16[64,800]{1,0:T(8,128)(2,1)} %get-tuple-element.14.c3_hbm, f32[6,400]{1,0:T(8,128)} %get-tuple-element.15.m1_hbm, f32[16,400]{1,0:T(8,128)} %get-tuple-element.16.m2_hbm, ...), custom_call_target="tpu_custom_call" | custom-call | flops 260000000 | bytes 11000000 | tf_op jit(solution)/shard_map/hours/pallas_call | solution.py:524
